TPU v7x, 32 devices: a whole 2x2x4 slice. The times are simulated.
32 devices in a mesh: dp: 8 (over z, y), fsdp: 4 (over x, core).
Axes of the slice: x: 2, y: 2, z: 4, core: 2. Of those that a mesh axis runs over, the one named last changes fastest.
Arguments:
- qkv_codes: bfloat16 [8, 4, 128, 3, 896], P('dp', 'fsdp'), may hold values from -4 to 4, as said below
- block_scales: bfloat16 [8, 4, 128, 3, 7], P('dp', 'fsdp'), may hold values from 0.25 to 2
- home_segments: int32 [8, 4, 128], P('dp', 'fsdp'), may hold values from -1 to 131, as said below
- kept_rows: int32 [8, 4], P('dp', 'fsdp'), may hold values from 32 to 64, as said below
- pack_list: int32 [8, 4, 4, 3], P(None, 'fsdp'), may hold values from 0 to 112, as said below
- w_out: bfloat16 [896, 1792], P('fsdp'), may hold values from -0.1875 to 0.1875
- cotangent: bfloat16 [8, 4, 128, 1792], P('dp', 'fsdp'), may hold values from -4 to 4
Outputs:
- output: bfloat16 [8, 4, 128, 1792], P('dp', 'fsdp')
- grad_codes: bfloat16 [8, 4, 128, 3, 896], P('dp', 'fsdp')
- grad_w_out: float32 [8, 896, 1792], P('dp', 'fsdp')
Inputs may be any that keep to these rules, and one draw needn't show every extreme that they name: Rows below kept_rows are whole images or the first part of one, and stay in place; the first image of every device has at least 3 rows. `pack_list`: one table for each fsdp index, the same on all its dp devices. Entry [s, d] describes the one whole image that dp index s sends to s + offset(d), offsets +1, -1, +2, -2, always inside the axis; length 0 means none, with the other entries 0. Lengths run from 3 to 16 and reach 16. Sent images lie at or above the source's kept_rows without intersection; placed images lie at or above the target's kept_rows without intersection, below 128. `home_segments`: kept rows carry their image number, runs of equal numbers; rows of the image sent in direction d carry 128 + d; other rows -1. `qkv_codes`: every entry is a value of the e4m3 8-bit float format.
All inputs are finite; a program needn't handle non-finite values.
Results may differ from a plain program's by a relative error of at most 0.02.
Values may be sent and summed in bfloat16 or wider, within the bound.
A program may use at most 64 MiB of HBM per device.

v0:
```python
import math

import jax
import jax.numpy as jnp
from jax import lax
from jax.sharding import PartitionSpec as P

HEADS = 8


offsets = (1, -1, 2, -2)


def shifted(block, axis, distance):
    devices = range(lax.axis_size(axis))
    route = [(i - distance, i) for i in devices if i - distance in devices]
    return lax.ppermute(block, axis, route)


def dequantize(codes, scales):
    count = codes.shape[0]
    blocks = scales.shape[-1]
    scaled = (
        codes.astype(jnp.float32).reshape(count, 3, blocks, -1)
        * scales.astype(jnp.float32)[..., None]
    )
    return scaled.reshape(count, 3, -1).astype(jnp.bfloat16)


def local_layer(codes, scales, labels, w_full, grad_out):
    count = codes.shape[0]
    width = w_full.shape[0]
    head_size = width // HEADS
    factor = 1.0 / math.sqrt(head_size)
    values = dequantize(codes, scales)
    query = values[:, 0].reshape(count, HEADS, head_size)
    keys = values[:, 1].reshape(count, HEADS, head_size)
    value_rows = values[:, 2].reshape(count, HEADS, head_size)
    scores = jnp.einsum("qhd,khd->hqk", query, keys, preferred_element_type=jnp.float32) * factor
    same = labels[:, None] == labels[None, :]
    scores = jnp.where(same[None], scores, -jnp.inf)
    top = jnp.max(scores, axis=-1, keepdims=True)
    weights = jnp.exp(scores - top)
    probs = weights / jnp.sum(weights, axis=-1, keepdims=True)
    probs_b = probs.astype(jnp.bfloat16)
    context = jnp.einsum("hqk,khd->qhd", probs_b, value_rows, preferred_element_type=jnp.float32)
    context = context.reshape(count, width).astype(jnp.bfloat16)
    output = jnp.dot(context, w_full, preferred_element_type=jnp.float32).astype(jnp.bfloat16)
    grad_context = lax.dot_general(
        grad_out, w_full, (((1,), (1,)), ((), ())), preferred_element_type=jnp.float32
    )
    grad_context = grad_context.astype(jnp.bfloat16).reshape(count, HEADS, head_size)
    grad_probs = jnp.einsum(
        "qhd,khd->hqk", grad_context, value_rows, preferred_element_type=jnp.float32
    )
    total = jnp.sum(probs * grad_probs, axis=-1, keepdims=True)
    grad_scores = (probs * (grad_probs - total) * factor).astype(jnp.bfloat16)
    grad_query = jnp.einsum("hqk,khd->qhd", grad_scores, keys, preferred_element_type=jnp.float32)
    grad_keys = jnp.einsum("hqk,qhd->khd", grad_scores, query, preferred_element_type=jnp.float32)
    grad_values = jnp.einsum(
        "hqk,qhd->khd", probs_b, grad_context, preferred_element_type=jnp.float32
    )
    grads = jnp.stack([grad_query, grad_keys, grad_values], axis=1).reshape(count, 3, -1)
    blocks = scales.shape[-1]
    grads = (grads.reshape(count, 3, blocks, -1) * scales.astype(jnp.float32)[..., None]).reshape(
        count, 3, -1
    )
    return (output, grads.astype(jnp.bfloat16), context)


def pad_rows(array, extra_rows, fill):
    extra = jnp.full((extra_rows,) + array.shape[1:], fill, array.dtype)
    return jnp.concatenate([array, extra], axis=0)


def cut_rows(buffer, at_row, length, slot):
    piece = lax.dynamic_slice_in_dim(buffer, at_row, slot, 0)
    present = (jnp.arange(slot) < length).reshape((slot,) + (1,) * (buffer.ndim - 1))
    return jnp.where(present, piece, jnp.zeros_like(piece))


def put_rows(buffer, piece, at_row, length):
    slot = piece.shape[0]
    old = lax.dynamic_slice_in_dim(buffer, at_row, slot, 0)
    present = (jnp.arange(slot) < length).reshape((slot,) + (1,) * (buffer.ndim - 1))
    return lax.dynamic_update_slice_in_dim(buffer, jnp.where(present, piece, old), at_row, 0)


def local(qkv_codes, block_scales, home_segments, kept_rows, pack_list, w_out, cotangent):
    position = lax.axis_index("dp")
    group_size = lax.axis_size("dp")
    codes = qkv_codes[0, 0]
    scales = block_scales[0, 0]
    segments = home_segments[0, 0]
    kept = kept_rows[0, 0]
    table = pack_list[:, 0]
    grad_out = cotangent[0, 0]
    row_count = codes.shape[0]
    slot = row_count // 8
    w_full = lax.all_gather(w_out, "fsdp", axis=0, tiled=True)
    inside = jnp.arange(row_count) < kept
    own_entries = lax.dynamic_index_in_dim(table, position, 0, keepdims=False)
    home_codes = pad_rows(codes, slot, 0)
    home_scales = pad_rows(scales, slot, 0)
    sent_codes = [
        cut_rows(home_codes, own_entries[route, 0], own_entries[route, 1], slot)
        for route in range(4)
    ]
    sent_scales = [
        cut_rows(home_scales, own_entries[route, 0], own_entries[route, 1], slot)
        for route in range(4)
    ]
    received = [
        shifted((sent_codes[route], sent_scales[route]), "dp", offsets[route]) for route in range(4)
    ]
    landing = []
    arrived = []
    for route in range(4):
        source = position - offsets[route]
        allowed = (source >= 0) & (source < group_size)
        entries = lax.dynamic_index_in_dim(
            table, jnp.clip(source, 0, group_size - 1), 0, keepdims=False
        )
        arrived.append(jnp.where(allowed, entries[route, 1], 0))
        landing.append(entries[route, 2])
    bal_codes = pad_rows(jnp.where(inside[:, None, None], codes, jnp.zeros_like(codes)), slot, 0)
    bal_scales = pad_rows(jnp.where(inside[:, None, None], scales, jnp.zeros_like(scales)), slot, 0)
    labels = pad_rows(jnp.where(inside, segments, -1), slot, -1)
    for route in range(4):
        bal_codes = put_rows(bal_codes, received[route][0], landing[route], arrived[route])
        bal_scales = put_rows(bal_scales, received[route][1], landing[route], arrived[route])
        marks = jnp.full((slot,), 100000 + route, jnp.int32)
        labels = put_rows(labels, marks, landing[route], arrived[route])
    output, grads, context = local_layer(
        bal_codes[:row_count], bal_scales[:row_count], labels[:row_count], w_full, grad_out
    )
    grads_padded = pad_rows(grads, slot, 0)
    going_back = [
        cut_rows(grads_padded, landing[route], arrived[route], slot) for route in range(4)
    ]
    returned = [shifted(going_back[route], "dp", -offsets[route]) for route in range(4)]
    home_grads = pad_rows(jnp.where(inside[:, None, None], grads, jnp.zeros_like(grads)), slot, 0)
    for route in range(4):
        home_grads = put_rows(
            home_grads, returned[route], own_entries[route, 0], own_entries[route, 1]
        )
    grad_codes = home_grads[:row_count]
    term = lax.dot_general(
        context, grad_out, (((0,), (0,)), ((), ())), preferred_element_type=jnp.float32
    )
    grad_w = lax.psum_scatter(
        term.astype(jnp.bfloat16), "fsdp", scatter_dimension=0, tiled=True
    ).astype(jnp.float32)
    return (output[None, None], grad_codes[None, None], grad_w[None])


def solution(mesh):
    return jax.shard_map(
        local,
        mesh=mesh,
        in_specs=(
            P("dp", "fsdp", None, None, None),
            P("dp", "fsdp", None, None, None),
            P("dp", "fsdp", None),
            P("dp", "fsdp"),
            P(None, "fsdp", None, None),
            P("fsdp", None),
            P("dp", "fsdp", None, None),
        ),
        out_specs=(
            P("dp", "fsdp", None, None),
            P("dp", "fsdp", None, None, None),
            P("dp", "fsdp", None),
        ),
        check_vma=False,
    )
```

profile of v0, /device:TPU:0, one launch (start us, length us, event | category | flops | bytes accessed | tf_op | source)
XLA Modules:
  0.0 216.1 jit_solution(17307450273464606200)
XLA Ops:
  14.0 1.4 copy.40
  20.4 2.0 fusion.21
  22.5 2.0 copy.43
  24.5 5.5 %collective-permute-start = (bf16[16,3,896]{2,0,1:T(8,128)(2,1)}, bf16[16,3,896]{2,0,1:T(8,128)(2,1)}, u32[]{:S(2)}, u32[]{:S(2)}) collective-permute-start(bf16[16,3,896]{2,0,1:T(8,128)(2,1)} %copy.43), channel_id=1, source_target_pairs={{0,4},{4,8},{8,12},{12,16},{16,20},{20,24},{24,28},{1,5},{5,9},{9,... | collective-permute-start | bytes 258056 | tf_op jit(solution)/shard_map/ppermute | solution.py:17
  32.5 5.5 %collective-permute-start.2 = (bf16[16,3,896]{2,0,1:T(8,128)(2,1)S(1)}, bf16[16,3,896]{2,0,1:T(8,128)(2,1)}, u32[]{:S(2)}, u32[]{:S(2)}) collective-permute-start(bf16[16,3,896]{2,0,1:T(8,128)(2,1)S(1)} %copy.49), channel_id=1, source_target_pairs={{0,8},{4,12},{8,16},{12,20},{16,24},{20,28},{1,9},{5,13},{9,17},{1... | collective-permute-start | bytes 258056 | tf_op jit(solution)/shard_map/ppermute | solution.py:17
  40.3 2.5 %collective-permute-start.4 = (bf16[16,3,7]{0,2,1:T(8,128)(2,1)}, bf16[16,3,7]{0,2,1:T(8,128)(2,1)S(1)}, u32[]{:S(2)}, u32[]{:S(2)}) collective-permute-start(bf16[16,3,7]{0,2,1:T(8,128)(2,1)} %get-tuple-element.24), channel_id=1, source_target_pairs={{0,4},{4,8},{8,12},{12,16},{16,20},{20,24},{24,28},{1,5},{5,9},{9,... | collective-permute-start | bytes 2024 | tf_op jit(solution)/shard_map/ppermute | solution.py:17
  61.0 5.1 %collective-permute-done.5 = bf16[16,3,7]{0,2,1:T(8,128)(2,1)S(1)} collective-permute-done((bf16[16,3,7]{0,2,1:T(8,128)(2,1)S(1)}, bf16[16,3,7]{0,2,1:T(8,128)(2,1)S(1)}, u32[]{:S(2)}, u32[]{:S(2)}) %collective-permute-start.5) | collective-permute-done | bytes 704 | tf_op jit(solution)/shard_map/ppermute | solution.py:17
  66.1 3.1 %collective-permute-start.6 = (bf16[16,3,7]{0,2,1:T(8,128)(2,1)S(1)}, bf16[16,3,7]{0,2,1:T(8,128)(2,1)S(1)}, u32[]{:S(2)}, u32[]{:S(2)}) collective-permute-start(bf16[16,3,7]{0,2,1:T(8,128)(2,1)S(1)} %copy-done.12), channel_id=1, source_target_pairs={{0,8},{4,12},{8,16},{12,20},{16,24},{20,28},{1,9},{5,13},{9,17},{1... | collective-permute-start | bytes 2024 | tf_op jit(solution)/shard_map/ppermute | solution.py:17
  70.5 1.5 collective-permute-start.7
  72.6 3.7 %collective-permute-done.7 = bf16[16,3,7]{0,2,1:T(8,128)(2,1)S(1)} collective-permute-done((bf16[16,3,7]{0,2,1:T(8,128)(2,1)S(1)}, bf16[16,3,7]{0,2,1:T(8,128)(2,1)S(1)}, u32[]{:S(2)}, u32[]{:S(2)}) %collective-permute-start.7) | collective-permute-done | bytes 704 | tf_op jit(solution)/shard_map/ppermute | solution.py:17
  76.9 2.0 copy.44
  78.9 1.4 dynamic-slice_select_fusion.7
  80.4 10.2 %dynamic_update_slice.48 = bf16[144,3,896]{0,2,1:T(8,128)(2,1)S(1)} dynamic-update-slice(bf16[144,3,896]{0,2,1:T(8,128)(2,1)S(1)} %concatenate.23, bf16[16,3,896]{0,2,1:T(8,128)(2,1)S(1)} %dynamic-slice_select_fusion.7, s32[]{:T(128)S(6)} %select_n.192, s32[]{:T(128)} %constant.53.clone.1, s32[]{:T(128)} %constant.53.clone.1) | dynamic-update-slice | bytes 172036 | tf_op jit(solution)/shard_map/dynamic_update_slice | solution.py:86
  92.2 10.2 %dynamic_update_slice.49 = bf16[144,3,896]{0,2,1:T(8,128)(2,1)S(1)} dynamic-update-slice(bf16[144,3,896]{0,2,1:T(8,128)(2,1)S(1)} %dynamic_update_slice.48, bf16[16,3,896]{0,2,1:T(8,128)(2,1)S(1)} %dynamic-slice_select_fusion.6, s32[]{:T(128)S(6)} %select_n.197, s32[]{:T(128)} %constant.53.clone.1, s32[]{:T(128)} %constant.53.clone.1) | dynamic-update-slice | bytes 172036 | tf_op jit(solution)/shard_map/dynamic_update_slice | solution.py:86
  104.0 10.2 %dynamic_update_slice.50 = bf16[144,3,896]{0,2,1:T(8,128)(2,1)S(1)} dynamic-update-slice(bf16[144,3,896]{0,2,1:T(8,128)(2,1)S(1)} %dynamic_update_slice.49, bf16[16,3,896]{0,2,1:T(8,128)(2,1)S(1)} %dynamic-slice_select_fusion.5, s32[]{:T(128)S(6)} %select_n.202, s32[]{:T(128)} %constant.53.clone.1, s32[]{:T(128)} %constant.53.clone.1) | dynamic-update-slice | bytes 172036 | tf_op jit(solution)/shard_map/dynamic_update_slice | solution.py:86
  115.0 10.2 %dynamic_update_slice.51 = bf16[144,3,896]{0,2,1:T(8,128)(2,1)S(1)} dynamic-update-slice(bf16[144,3,896]{0,2,1:T(8,128)(2,1)S(1)} %dynamic_update_slice.50, bf16[16,3,896]{0,2,1:T(8,128)(2,1)S(1)} %dynamic-slice_select_fusion.4, s32[]{:T(128)S(6)} %select_n.207, s32[]{:T(128)} %constant.53.clone.1, s32[]{:T(128)} %constant.53.clone.1) | dynamic-update-slice | bytes 172036 | tf_op jit(solution)/shard_map/dynamic_update_slice | solution.py:86
  127.1 2.7 %convolution_convert_fusion = bf16[896,1792]{1,0:T(8,128)(2,1)} fusion(bf16[128,896]{0,1:T(8,128)(2,1)S(1)} %bitcast.87, bf16[1,1,128,1792]{3,2,1,0:T(8,128)(2,1)S(1)} %copy-done), kind=kOutput, calls=%fused_computation.2 | convolution fusion | flops 412647424 | bytes 3899392 | tf_op jit(solution)/shard_map/dot_general | solution.py:148
  129.8 3.0 %convolution_convert_fusion.2 = bf16[128,896]{1,0:T(8,128)(2,1)S(1)} fusion(bf16[896,1792]{1,0:T(8,128)(2,1)} %all-gather.2.cloned.1.call-done, bf16[1,1,128,1792]{3,2,1,0:T(8,128)(2,1)S(1)} %copy-done), kind=kOutput, calls=%fused_computation.25 | convolution fusion | flops 411156480 | bytes 3899392 | tf_op jit(solution)/shard_map/dot_general | solution.py:49
  133.3 1.7 fusion.12
  135.0 1.8 fusion.13
  138.1 2.0 fusion.25
  140.1 2.0 copy.59
  142.1 1.5 collective-permute-start.8
  144.5 5.9 %collective-permute-start.9 = (bf16[16,3,896]{2,0,1:T(8,128)(2,1)}, bf16[16,3,896]{2,0,1:T(8,128)(2,1)}, u32[]{:S(2)}, u32[]{:S(2)}) collective-permute-start(bf16[16,3,896]{2,0,1:T(8,128)(2,1)} %copy.61), channel_id=1, source_target_pairs={{0,4},{4,8},{8,12},{12,16},{16,20},{20,24},{24,28},{1,5},{5,9},{9,... | collective-permute-start | bytes 258056 | tf_op jit(solution)/shard_map/ppermute | solution.py:17
  152.8 5.2 %collective-permute-start.11 = (bf16[16,3,896]{2,0,1:T(8,128)(2,1)S(1)}, bf16[16,3,896]{2,0,1:T(8,128)(2,1)}, u32[]{:S(2)}, u32[]{:S(2)}) collective-permute-start(bf16[16,3,896]{2,0,1:T(8,128)(2,1)S(1)} %copy.65), channel_id=1, source_target_pairs={{0,8},{4,12},{8,16},{12,20},{16,24},{20,28},{1,9},{5,13},{9,17},{1... | collective-permute-start | bytes 258056 | tf_op jit(solution)/shard_map/ppermute | solution.py:17
  158.0 3.4 %fusion.2 = bf16[1,1,128,1792]{3,2,1,0:T(8,128)(2,1)} fusion(bf16[128,896]{0,1:T(8,128)(2,1)S(1)} %bitcast.88, bf16[896,1792]{1,0:T(8,128)(2,1)} %all-gather.2.cloned.1.call-done), kind=kOutput, calls=%fused_computation.4 | convolution fusion | flops 411271168 | bytes 3899392 | tf_op jit(solution)/shard_map/dot_general | solution.py:48
  161.5 2.0 copy.60
  164.9 10.2 %dynamic_update_slice.60 = bf16[144,3,896]{0,2,1:T(8,128)(2,1)S(1)} dynamic-update-slice(bf16[144,3,896]{0,2,1:T(8,128)(2,1)S(1)} %concatenate.28, bf16[16,3,896]{0,2,1:T(8,128)(2,1)S(1)} %dynamic-slice_select_fusion.3, s32[]{:T(128)S(6)} %select_n.190, s32[]{:T(128)} %constant.53.clone.1, s32[]{:T(128)} %constant.53.clone.1) | dynamic-update-slice | bytes 172036 | tf_op jit(solution)/shard_map/dynamic_update_slice | solution.py:86
  176.8 7.7 %dynamic_update_slice.61 = bf16[144,3,896]{0,2,1:T(8,128)(2,1)S(1)} dynamic-update-slice(bf16[144,3,896]{0,2,1:T(8,128)(2,1)S(1)} %dynamic_update_slice.60, bf16[16,3,896]{0,2,1:T(8,128)(2,1)S(1)} %dynamic-slice_select_fusion.2, s32[]{:T(128)S(6)} %select_n.195, s32[]{:T(128)} %constant.53.clone.1, s32[]{:T(128)} %constant.53.clone.1) | dynamic-update-slice | bytes 172036 | tf_op jit(solution)/shard_map/dynamic_update_slice | solution.py:86
  186.1 10.2 %dynamic_update_slice.62 = bf16[144,3,896]{0,2,1:T(8,128)(2,1)S(1)} dynamic-update-slice(bf16[144,3,896]{0,2,1:T(8,128)(2,1)S(1)} %dynamic_update_slice.61, bf16[16,3,896]{0,2,1:T(8,128)(2,1)S(1)} %dynamic-slice_select_fusion.1, s32[]{:T(128)S(6)} %select_n.200, s32[]{:T(128)} %constant.53.clone.1, s32[]{:T(128)} %constant.53.clone.1) | dynamic-update-slice | bytes 172036 | tf_op jit(solution)/shard_map/dynamic_update_slice | solution.py:86
  197.9 7.7 %dynamic_update_slice.63 = bf16[144,3,896]{0,2,1:T(8,128)(2,1)S(1)} dynamic-update-slice(bf16[144,3,896]{0,2,1:T(8,128)(2,1)S(1)} %dynamic_update_slice.62, bf16[16,3,896]{0,2,1:T(8,128)(2,1)S(1)} %dynamic-slice_select_fusion, s32[]{:T(128)S(6)} %select_n.205, s32[]{:T(128)} %constant.53.clone.1, s32[]{:T(128)} %constant.53.clone.1) | dynamic-update-slice | bytes 172036 | tf_op jit(solution)/shard_map/dynamic_update_slice | solution.py:86
  206.9 2.4 %bitcast_convert_fusion = f32[1,224,1792]{2,1,0:T(8,128)} fusion(bf16[224,1792]{1,0:T(8,128)(2,1)} %reduce-scatter.2.cloned.1.call-done), kind=kLoop, calls=%fused_computation.32 | loop fusion | flops 401408 | bytes 2408448 | tf_op jit(solution)/shard_map/broadcast_in_dim | solution.py:154
  (144 shorter events, 37.2 us)
Async XLA Ops:
  7.2 119.9 %copy-start = (bf16[1,1,128,1792]{3,2,1,0:T(8,128)(2,1)S(1)}, bf16[1,1,128,1792]{3,2,1,0:T(8,128)(2,1)}, u32[]{:S(2)}) copy-start(bf16[1,1,128,1792]{3,2,1,0:T(8,128)(2,1)} %param.13) | copy-start | bytes 1376260
  7.2 122.6 %all-gather.2.cloned.1.call-start = ((), (), s32[]{:S(2)}) async-start(), calls=%async_computation.1 | async-start | bytes 4014080 | tf_op jit(solution)/shard_map/all_gather | solution.py:100
  17.3 22.3 %copy-start.4 = (pred[16]{0:T(512)(128)(4,1)}, pred[16]{0:T(512)(128)(4,1)S(1)}, u32[]{:S(2)}) copy-start(pred[16]{0:T(512)(128)(4,1)S(1)} %get-tuple-element.49) | copy-start | bytes 52
  17.3 22.3 %copy-start.6 = (pred[16]{0:T(512)(128)(4,1)}, pred[16]{0:T(512)(128)(4,1)S(1)}, u32[]{:S(2)}) copy-start(pred[16]{0:T(512)(128)(4,1)S(1)} %get-tuple-element.50) | copy-start | bytes 52
  19.8 19.8 %copy-start.8 = (pred[16]{0:T(512)(128)(4,1)}, pred[16]{0:T(512)(128)(4,1)S(1)}, u32[]{:S(2)}) copy-start(pred[16]{0:T(512)(128)(4,1)S(1)} %get-tuple-element.51) | copy-start | bytes 52
  19.9 19.8 %copy-start.10 = (pred[16]{0:T(512)(128)(4,1)}, pred[16]{0:T(512)(128)(4,1)S(1)}, u32[]{:S(2)}) copy-start(pred[16]{0:T(512)(128)(4,1)S(1)} %get-tuple-element.52) | copy-start | bytes 52
  22.5 17.2 %copy-start.3 = (bf16[1,1,128,3,7]{2,4,3,1,0:T(8,128)(2,1)S(1)}, bf16[1,1,128,3,7]{2,4,3,1,0:T(8,128)(2,1)}, u32[]{:S(2)}) copy-start(bf16[1,1,128,3,7]{2,4,3,1,0:T(8,128)(2,1)} %param.8) | copy-start | bytes 16132
  24.5 52.4 %collective-permute-start = (bf16[16,3,896]{2,0,1:T(8,128)(2,1)}, bf16[16,3,896]{2,0,1:T(8,128)(2,1)}, u32[]{:S(2)}, u32[]{:S(2)}) collective-permute-start(bf16[16,3,896]{2,0,1:T(8,128)(2,1)} %copy.43), channel_id=1, source_target_pairs={{0,4},{4,8},{8,12},{12,16},{16,20},{20,24},{24,28},{1,5},{5,9},{9,... | collective-permute-start | bytes 258056 | tf_op jit(solution)/shard_map/ppermute | solution.py:17
  30.8 21.0 %copy-start.26 = (s32[1,1,128]{2,1,0:T(1,128)S(1)}, s32[1,1,128]{2,1,0:T(1,128)}, u32[]{:S(2)}) copy-start(s32[1,1,128]{2,1,0:T(1,128)} %param.9) | copy-start | bytes 1540
  30.8 59.7 %collective-permute-start.1 = (bf16[16,3,896]{2,0,1:T(8,128)(2,1)}, bf16[16,3,896]{2,0,1:T(8,128)(2,1)}, u32[]{:S(2)}, u32[]{:S(2)}) collective-permute-start(bf16[16,3,896]{2,0,1:T(8,128)(2,1)} %copy.46), channel_id=1, source_target_pairs={{4,0},{8,4},{12,8},{16,12},{20,16},{24,20},{28,24},{5,1},{9,5},{13... | collective-permute-start | bytes 258056 | tf_op jit(solution)/shard_map/ppermute | solution.py:17
  32.5 69.9 %collective-permute-start.2 = (bf16[16,3,896]{2,0,1:T(8,128)(2,1)S(1)}, bf16[16,3,896]{2,0,1:T(8,128)(2,1)}, u32[]{:S(2)}, u32[]{:S(2)}) collective-permute-start(bf16[16,3,896]{2,0,1:T(8,128)(2,1)S(1)} %copy.49), channel_id=1, source_target_pairs={{0,8},{4,12},{8,16},{12,20},{16,24},{20,28},{1,9},{5,13},{9,17},{1... | collective-permute-start | bytes 258056 | tf_op jit(solution)/shard_map/ppermute | solution.py:17
  38.3 75.9 %collective-permute-start.3 = (bf16[16,3,896]{2,0,1:T(8,128)(2,1)S(1)}, bf16[16,3,896]{2,0,1:T(8,128)(2,1)S(1)}, u32[]{:S(2)}, u32[]{:S(2)}) collective-permute-start(bf16[16,3,896]{2,0,1:T(8,128)(2,1)S(1)} %copy.52), channel_id=1, source_target_pairs={{8,0},{12,4},{16,8},{20,12},{24,16},{28,20},{9,1},{13,5},{17,9},{2... | collective-permute-start | bytes 258056 | tf_op jit(solution)/shard_map/ppermute | solution.py:17
  40.3 18.6 %collective-permute-start.4 = (bf16[16,3,7]{0,2,1:T(8,128)(2,1)}, bf16[16,3,7]{0,2,1:T(8,128)(2,1)S(1)}, u32[]{:S(2)}, u32[]{:S(2)}) collective-permute-start(bf16[16,3,7]{0,2,1:T(8,128)(2,1)} %get-tuple-element.24), channel_id=1, source_target_pairs={{0,4},{4,8},{8,12},{12,16},{16,20},{20,24},{24,28},{1,5},{5,9},{9,... | collective-permute-start | bytes 2024 | tf_op jit(solution)/shard_map/ppermute | solution.py:17
  42.9 164.0 %reduce-scatter.2.cloned.1.call-start = ((), (), s32[]{:S(2)}) async-start(), calls=%async_computation.2 | async-start | bytes 4014080 | tf_op jit(solution)/shard_map/reduce_scatter | solution.py:151
  57.7 21.2 %copy-start.16 = (pred[16]{0:T(512)(128)(4,1)}, pred[16]{0:T(512)(128)(4,1)S(1)}, u32[]{:S(2)}) copy-start(pred[16]{0:T(512)(128)(4,1)S(1)} %iota_compare_fusion.7) | copy-start | bytes 52
  57.7 11.5 %copy-start.18 = (pred[16]{0:T(512)(128)(4,1)}, pred[16]{0:T(512)(128)(4,1)S(1)}, u32[]{:S(2)}) copy-start(pred[16]{0:T(512)(128)(4,1)S(1)} %iota_compare_fusion.5) | copy-start | bytes 52
  58.4 13.5 %copy-start.21 = (pred[16]{0:T(512)(128)(4,1)S(1)}, pred[16]{0:T(512)(128)(4,1)}, u32[]{:S(2)}) copy-start(pred[16]{0:T(512)(128)(4,1)} %iota_compare_fusion.3) | copy-start | bytes 52
  58.8 18.1 %copy-start.24 = (pred[16]{0:T(512)(128)(4,1)}, pred[16]{0:T(512)(128)(4,1)S(1)}, u32[]{:S(2)}) copy-start(pred[16]{0:T(512)(128)(4,1)S(1)} %iota_compare_fusion.1) | copy-start | bytes 52
  59.1 7.0 %collective-permute-start.5 = (bf16[16,3,7]{0,2,1:T(8,128)(2,1)S(1)}, bf16[16,3,7]{0,2,1:T(8,128)(2,1)S(1)}, u32[]{:S(2)}, u32[]{:S(2)}) collective-permute-start(bf16[16,3,7]{0,2,1:T(8,128)(2,1)S(1)} %copy-done.13), channel_id=1, source_target_pairs={{4,0},{8,4},{12,8},{16,12},{20,16},{24,20},{28,24},{5,1},{9,5},{13... | collective-permute-start | bytes 2024 | tf_op jit(solution)/shard_map/ppermute | solution.py:17
  66.1 4.4 %collective-permute-start.6 = (bf16[16,3,7]{0,2,1:T(8,128)(2,1)S(1)}, bf16[16,3,7]{0,2,1:T(8,128)(2,1)S(1)}, u32[]{:S(2)}, u32[]{:S(2)}) collective-permute-start(bf16[16,3,7]{0,2,1:T(8,128)(2,1)S(1)} %copy-done.12), channel_id=1, source_target_pairs={{0,8},{4,12},{8,16},{12,20},{16,24},{20,28},{1,9},{5,13},{9,17},{1... | collective-permute-start | bytes 2024 | tf_op jit(solution)/shard_map/ppermute | solution.py:17
  70.5 5.8 %collective-permute-start.7 = (bf16[16,3,7]{0,2,1:T(8,128)(2,1)S(1)}, bf16[16,3,7]{0,2,1:T(8,128)(2,1)S(1)}, u32[]{:S(2)}, u32[]{:S(2)}) collective-permute-start(bf16[16,3,7]{0,2,1:T(8,128)(2,1)S(1)} %get-tuple-element.22), channel_id=1, source_target_pairs={{8,0},{12,4},{16,8},{20,12},{24,16},{28,20},{9,1},{13,5},{17,9},{2... | collective-permute-start | bytes 2024 | tf_op jit(solution)/shard_map/ppermute | solution.py:17
  80.4 11.5 %copy-start.19 = (pred[16]{0:T(512)(128)(4,1)S(1)}, pred[16]{0:T(512)(128)(4,1)}, u32[]{:S(2)}) copy-start(pred[16]{0:T(512)(128)(4,1)} %copy-done.18) | copy-start | bytes 52
  92.2 11.5 %copy-start.22 = (pred[16]{0:T(512)(128)(4,1)S(1)}, pred[16]{0:T(512)(128)(4,1)}, u32[]{:S(2)}) copy-start(pred[16]{0:T(512)(128)(4,1)} %iota_compare_fusion.3) | copy-start | bytes 52
  104.0 10.6 %copy-start.25 = (pred[16]{0:T(512)(128)(4,1)S(1)}, pred[16]{0:T(512)(128)(4,1)}, u32[]{:S(2)}) copy-start(pred[16]{0:T(512)(128)(4,1)} %copy-done.24) | copy-start | bytes 52
  125.4 8.0 %copy-start.1 = (bf16[128,1,896]{0,2,1:T(8,128)(2,1)}, bf16[128,1,896]{0,2,1:T(8,128)(2,1)S(1)}, u32[]{:S(2)}) copy-start(bf16[128,1,896]{0,2,1:T(8,128)(2,1)S(1)} %get-tuple-element.16) | copy-start | bytes 688132
  142.1 19.4 %collective-permute-start.8 = (bf16[16,3,896]{2,0,1:T(8,128)(2,1)}, bf16[16,3,896]{2,0,1:T(8,128)(2,1)}, u32[]{:S(2)}, u32[]{:S(2)}) collective-permute-start(bf16[16,3,896]{2,0,1:T(8,128)(2,1)} %copy.59), channel_id=1, source_target_pairs={{4,0},{8,4},{12,8},{16,12},{20,16},{24,20},{28,24},{5,1},{9,5},{13... | collective-permute-start | bytes 258056 | tf_op jit(solution)/shard_map/ppermute | solution.py:17
  144.5 30.6 %collective-permute-start.9 = (bf16[16,3,896]{2,0,1:T(8,128)(2,1)}, bf16[16,3,896]{2,0,1:T(8,128)(2,1)}, u32[]{:S(2)}, u32[]{:S(2)}) collective-permute-start(bf16[16,3,896]{2,0,1:T(8,128)(2,1)} %copy.61), channel_id=1, source_target_pairs={{0,4},{4,8},{8,12},{12,16},{16,20},{20,24},{24,28},{1,5},{5,9},{9,... | collective-permute-start | bytes 258056 | tf_op jit(solution)/shard_map/ppermute | solution.py:17
  151.2 33.2 %collective-permute-start.10 = (bf16[16,3,896]{2,0,1:T(8,128)(2,1)}, bf16[16,3,896]{2,0,1:T(8,128)(2,1)}, u32[]{:S(2)}, u32[]{:S(2)}) collective-permute-start(bf16[16,3,896]{2,0,1:T(8,128)(2,1)} %copy.63), channel_id=1, source_target_pairs={{8,0},{12,4},{16,8},{20,12},{24,16},{28,20},{9,1},{13,5},{17,9},{2... | collective-permute-start | bytes 258056 | tf_op jit(solution)/shard_map/ppermute | solution.py:17
  152.8 43.5 %collective-permute-start.11 = (bf16[16,3,896]{2,0,1:T(8,128)(2,1)S(1)}, bf16[16,3,896]{2,0,1:T(8,128)(2,1)}, u32[]{:S(2)}, u32[]{:S(2)}) collective-permute-start(bf16[16,3,896]{2,0,1:T(8,128)(2,1)S(1)} %copy.65), channel_id=1, source_target_pairs={{0,8},{4,12},{8,16},{12,20},{16,24},{20,28},{1,9},{5,13},{9,17},{1... | collective-permute-start | bytes 258056 | tf_op jit(solution)/shard_map/ppermute | solution.py:17
  164.9 11.5 %copy-start.9 = (pred[16]{0:T(512)(128)(4,1)S(1)}, pred[16]{0:T(512)(128)(4,1)}, u32[]{:S(2)}) copy-start(pred[16]{0:T(512)(128)(4,1)} %copy-done.8) | copy-start | bytes 52
  176.8 9.0 %copy-start.7 = (pred[16]{0:T(512)(128)(4,1)S(1)}, pred[16]{0:T(512)(128)(4,1)}, u32[]{:S(2)}) copy-start(pred[16]{0:T(512)(128)(4,1)} %copy-done.6) | copy-start | bytes 52
  186.1 11.5 %copy-start.5 = (pred[16]{0:T(512)(128)(4,1)S(1)}, pred[16]{0:T(512)(128)(4,1)}, u32[]{:S(2)}) copy-start(pred[16]{0:T(512)(128)(4,1)} %copy-done.4) | copy-start | bytes 52
  (9 other events, 15.4 us)
Sparse Core Ops, SparseCore 0:
  43.0 30.5 all-gather.1
  129.9 36.7 reduce-scatter.1
where the time goes:
time: 220 us; the launch traced here: 216 us
  local copies, waits for them, and re-layouts  106 us (48%)
  starting transfers between devices  36 us (16%)
  between operations  33.2 us (15%)
  other arithmetic  16.7 us (8%)
  matrix products  15.1 us (7%)
  waiting for transfers between devices  9.6 us (4%)
    dynamic_update_slice x12, local copies, waits for them, and re-layouts, put_rows(): lax.dynamic_update_slice_in_dim(buffer, jnp.where(present, piece, old), a...  78.5 us
    ppermute x12, starting transfers between devices, shifted(): return lax.ppermute(block, axis, route)  35.9 us
    ppermute x8, local copies, waits for them, and re-layouts, shifted(): return lax.ppermute(block, axis, route)  10.7 us
    ppermute x12, waiting for transfers between devices, shifted(): return lax.ppermute(block, axis, route)  9.55 us
    select_n x8, local copies, waits for them, and re-layouts, cut_rows(): return jnp.where(present, piece, jnp.zeros_like(piece))  7.34 us
    select_n x12, other arithmetic, put_rows(): jnp.where(present, piece, old)  5.34 us
    select_n x3, other arithmetic, cut_rows(): return jnp.where(present, piece, jnp.zeros_like(piece))  4.74 us
  transfers between devices with their start and end apart: 14, of which 3 were waited for; matrix products, arithmetic and copies ran while one was open for 57% of the time, Pallas kernels for 0%

commit v1 on v0

--- a/solution.py
+++ b/solution.py
@@ -1,8 +1,11 @@
+import functools
 import math
 
 import jax
 import jax.numpy as jnp
 from jax import lax
+from jax.experimental import pallas as pl
+from jax.experimental.pallas import tpu as pltpu
 from jax.sharding import PartitionSpec as P
 
 HEADS = 8
@@ -154,9 +157,387 @@
     return (output[None, None], grad_codes[None, None], grad_w[None])
 
 
+BF = jnp.bfloat16
+F32 = jnp.float32
+PAIR = 256
+
+
+def iota(shape, dim):
+    return lax.broadcasted_iota(jnp.int32, shape, dim)
+
+
+def hot(mask):
+    return mask.astype(F32).astype(BF)
+
+
+def mm(a, b, dims=((1,), (0,))):
+    return lax.dot_general(a, b, (dims, ((), ())), preferred_element_type=F32)
+
+
+def window(block, share):
+    low = block * share // 128 * 128
+    high = -(-(block + 1) * share // 128) * 128
+    return low, high
+
+
+def heads_kernel(
+    groups, share, width,
+    table, kept_ref, seg_ref, x_ref, w_ref, cot_ref,
+    out_ref, grad_ref, gw_ref,
+    img_send, img_recv, w_pad, cot_all, bal, qkv, scl, probs,
+    ctx_send, ctx_all, gc_send, gc_in, part_send, part_in, x_send, x_in,
+    packed, nat, back_send, back_recv,
+    cot_s, cot_r, fwd_s, fwd_r, img_s, img_r, ctx_s, ctx_r, gc_s, gc_r,
+    part_s, part_r, xs_s, xs_r, back_s, back_r,
+):
+    pos = lax.axis_index("dp")
+    me = lax.axis_index("fsdp")
+    sib = me + 1 - 2 * (me % 2)
+    cross = (me + 2) % 4
+    diag = (sib + 2) % 4
+    peer = (me, sib, cross, diag)
+    rows = cot_ref.shape[0]
+    slot = img_send.shape[0] // 4
+    feats = 3 * width
+    model = cot_ref.shape[1]
+    half = model // 2
+    head = width // HEADS
+    factor = 1.0 / math.sqrt(head)
+
+    def remote(src, dst, s, r, where):
+        return pltpu.make_async_remote_copy(
+            src_ref=src, dst_ref=dst, send_sem=s, recv_sem=r,
+            device_id=where, device_id_type=pl.DeviceIdType.MESH,
+        )
+
+    def at_dp(index):
+        return (index, me)
+
+    def at_fsdp(index):
+        return (pos, index)
+
+    img_recv[...] = jnp.zeros_like(img_recv)
+    back_recv[...] = jnp.zeros_like(back_recv)
+
+    barrier = pltpu.get_barrier_semaphore()
+    for r in (1, 2, 3):
+        pl.semaphore_signal(barrier, inc=1, device_id=at_fsdp(peer[r]),
+                            device_id_type=pl.DeviceIdType.MESH)
+    valid_to = [(pos + o >= 0) & (pos + o < groups) for o in offsets]
+    valid_from = [(pos - o >= 0) & (pos - o < groups) for o in offsets]
+    for d in range(4):
+        @pl.when(valid_to[d])
+        def _(d=d):
+            pl.semaphore_signal(barrier, inc=1, device_id=at_dp(pos + offsets[d]),
+                                device_id_type=pl.DeviceIdType.MESH)
+    pl.semaphore_wait(barrier, 3 + jnp.minimum(pos, 2) + jnp.minimum(groups - 1 - pos, 2))
+
+    hr = rows // 2
+    cot_out = []
+    for c in range(2):
+        part = pl.ds(c * hr, hr)
+        cot_out.append(remote(cot_ref.at[part], cot_all.at[1, part], cot_s.at[c], cot_r.at[c],
+                              at_fsdp(cross)))
+    cot_sib = remote(cot_ref, cot_all.at[0], cot_s.at[2], cot_r.at[2], at_fsdp(sib))
+    cot_out[0].start()
+    cot_out[1].start()
+    cot_sib.start()
+    forward = [
+        remote(cot_all.at[1, pl.ds(c * hr, hr)], cot_all.at[2, pl.ds(c * hr, hr)],
+               fwd_s.at[c], fwd_r.at[c], at_fsdp(sib))
+        for c in range(2)
+    ]
+
+    kept = kept_ref[0, 0]
+    r64 = iota((4 * slot, rows), 0)
+    c64 = iota((4 * slot, rows), 1)
+
+    def selection(starts, lengths):
+        mask = jnp.zeros((4 * slot, rows), F32)
+        for d in range(4):
+            step = r64 - d * slot
+            ok = (step >= 0) & (step < lengths[d]) & (step < slot) & (c64 == starts[d] + step)
+            mask = mask + ok.astype(F32)
+        return mask.astype(BF)
+
+    own_start = [table[pos, 3 * d] for d in range(4)]
+    own_len = [table[pos, 3 * d + 1] for d in range(4)]
+    landing, arrived = [], []
+    for d in range(4):
+        src = jnp.clip(pos - offsets[d], 0, groups - 1)
+        landing.append(table[src, 3 * d + 2])
+        arrived.append(jnp.where(valid_from[d], table[src, 3 * d + 1], 0))
+    img_send[...] = mm(selection(own_start, own_len), x_ref[...]).astype(BF)
+    images = []
+    for d in range(4):
+        part = pl.ds(d * slot, slot)
+        images.append(remote(img_send.at[part], img_recv.at[part], img_s.at[d], img_r.at[d],
+                             at_dp(jnp.clip(pos + offsets[d], 0, groups - 1))))
+
+        @pl.when(valid_to[d])
+        def _(d=d):
+            images[d].start()
+
+    w_pad[0:share] = w_ref[...]
+    w_pad[share:PAIR] = jnp.zeros((PAIR - share, model), BF)
+    gc_in[0] = mm(cot_ref[...], w_pad[...], ((1,), (1,))).astype(BF)
+
+    rr = iota((rows, rows), 0)
+    cc = iota((rows, rows), 1)
+    keep_hot = hot((rr == cc) & (rr < kept))
+
+    def placing(starts, lengths):
+        r_ = iota((rows, 4 * slot), 0)
+        c_ = iota((rows, 4 * slot), 1)
+        mask = jnp.zeros((rows, 4 * slot), F32)
+        for d in range(4):
+            step = c_ - d * slot
+            ok = (step >= 0) & (step < lengths[d]) & (step < slot) & (r_ == starts[d] + step)
+            mask = mask + ok.astype(F32)
+        return mask.astype(BF)
+
+    row_id = iota((1, rows), 1)
+    marks = jnp.where(row_id < kept, seg_ref[...], -1)
+    for d in range(4):
+        here = (row_id >= landing[d]) & (row_id < landing[d] + arrived[d])
+        marks = jnp.where(here, 100000 + d, marks)
+    marks_row = jnp.broadcast_to(marks.astype(F32), (rows, rows))
+    marks_col = jnp.sum(jnp.where(rr == cc, marks_row, 0.0), axis=1, keepdims=True)
+    same = marks_col == marks_row
+    bias = jnp.where(same, 0.0, -jnp.inf)
+    bias2 = jnp.concatenate([bias, bias], axis=0)
+
+    for d in range(4):
+        @pl.when(valid_from[d])
+        def _(d=d):
+            images[d].wait_recv()
+    place = placing(landing, arrived)
+    bal[...] = (mm(keep_hot, x_ref[...]) + mm(place, img_recv[...])).astype(BF)
+
+    lanes = iota((1, PAIR), 1)
+    first = hot(lanes < head)
+    second = hot(lanes >= head)
+    for j in range(4):
+        low, high = window(j, share)
+        pick = hot((iota((high - low, PAIR), 0) + low == iota((high - low, PAIR), 1) + j * share)
+                   & (iota((high - low, PAIR), 1) < share))
+        block = (iota((128, PAIR), 1) + j * share) // 128
+        for m in range(3):
+            values = mm(bal[:, m * width + low:m * width + high], pick)
+            spread = hot((iota((128, PAIR), 0) == block + m * (width // 128))
+                         & (iota((128, PAIR), 1) < share))
+            scale = mm(bal[:, feats:feats + 128], spread)
+            scl[m * 4 + j] = scale.astype(BF)
+            qkv[m * 4 + j] = (values * scale).astype(BF)
+
+    def stack(x):
+        return jnp.concatenate([x * first, x * second], axis=0)
+
+    def wide(x):
+        return jnp.concatenate([x[:rows], x[rows:]], axis=1)
+
+    ctx_out = [None] * 4
+    for r in (2, 3, 1, 0):
+        j = peer[r]
+        scores = mm(stack(qkv[j]), qkv[4 + j], ((1,), (1,))) * factor + bias2
+        top = jnp.max(scores, axis=-1, keepdims=True)
+        weights = jnp.exp(scores - top)
+        p = weights / jnp.sum(weights, axis=-1, keepdims=True)
+        probs[r] = p
+        ctx = mm(wide(p.astype(BF)), stack(qkv[8 + j])).astype(BF)
+        if r == 0:
+            ctx_all[0] = ctx
+        else:
+            ctx_send[r] = ctx
+            ctx_out[r] = remote(ctx_send.at[r], ctx_all.at[r], ctx_s.at[r], ctx_r.at[r],
+                                at_fsdp(j))
+            ctx_out[r].start()
+
+    gc_out = [None] * 4
+
+    def send_gc(r):
+        gc_send[r] = mm(cot_all[r - 1], w_pad[...], ((1,), (1,))).astype(BF)
+        gc_out[r] = remote(gc_send.at[r], gc_in.at[r], gc_s.at[r], gc_r.at[r], at_fsdp(peer[r]))
+        gc_out[r].start()
+
+    cot_sib.wait_recv()
+    for c in range(2):
+        cot_out[c].wait_recv()
+        forward[c].start()
+    send_gc(2)
+    send_gc(1)
+    for c in range(2):
+        forward[c].wait_recv()
+    send_gc(3)
+
+    def product(r, c):
+        return mm(ctx_all[r], w_pad[:, c * half:(c + 1) * half])
+
+    sent = []
+    crossing = []
+    ctx_out[3].wait_recv()
+    for c in range(2):
+        part_send[c] = product(3, c).astype(BF)
+        sent.append(remote(part_send.at[c], part_in.at[c], part_s.at[c], part_r.at[c],
+                           at_fsdp(sib)))
+        sent[c].start()
+    ctx_out[2].wait_recv()
+    for c in range(2):
+        own = product(2, c)
+        sent[c].wait_recv()
+        x_send[c] = (own + part_in[c].astype(F32)).astype(BF)
+        crossing.append(remote(x_send.at[c], x_in.at[c], xs_s.at[c], xs_r.at[c], at_fsdp(cross)))
+        crossing[c].start()
+    ctx_out[1].wait_recv()
+    for c in range(2):
+        part_send[2 + c] = product(1, c).astype(BF)
+        sent.append(remote(part_send.at[2 + c], part_in.at[2 + c], part_s.at[2 + c],
+                           part_r.at[2 + c], at_fsdp(sib)))
+        sent[2 + c].start()
+
+    for r in (0, 1, 2, 3):
+        j = peer[r]
+        if r:
+            gc_out[r].wait_recv()
+        p = probs[r]
+        gstack = stack(gc_in[r])
+        gp = mm(gstack, qkv[8 + j], ((1,), (1,)))
+        total = jnp.sum(p * gp, axis=-1, keepdims=True)
+        gs = (p * (gp - total) * factor).astype(BF)
+        gq = mm(wide(gs), stack(qkv[4 + j]))
+        gk = mm(gs, stack(qkv[j]), ((0,), (0,)))
+        gv = mm(p.astype(BF), gstack, ((0,), (0,)))
+        for m, g in enumerate((gq, gk, gv)):
+            packed[m * 4 + j] = (g * scl[m * 4 + j].astype(F32)).astype(BF)
+    for m in range(3):
+        blocks = [None] * (width // 128)
+        for j in range(4):
+            low, high = window(j, share)
+            spread = hot((iota((PAIR, high - low), 1) + low
+                          == iota((PAIR, high - low), 0) + j * share)
+                         & (iota((PAIR, high - low), 0) < share))
+            piece = mm(packed[m * 4 + j], spread)
+            for b in range((high - low) // 128):
+                add = piece[:, b * 128:(b + 1) * 128]
+                at = low // 128 + b
+                blocks[at] = add if blocks[at] is None else blocks[at] + add
+        for b in range(width // 128):
+            nat[:, m * width + b * 128:m * width + (b + 1) * 128] = blocks[b].astype(BF)
+
+    back_send[...] = mm(selection(landing, arrived), nat[...]).astype(BF)
+    returns = []
+    for d in range(4):
+        part = pl.ds(d * slot, slot)
+        returns.append(remote(back_send.at[part], back_recv.at[part], back_s.at[d], back_r.at[d],
+                              at_dp(jnp.clip(pos - offsets[d], 0, groups - 1))))
+
+        @pl.when(valid_from[d])
+        def _(d=d):
+            returns[d].start()
+
+    acc = mm(ctx_all[0], cot_ref[...], ((0,), (0,)))
+    for r in (1, 2, 3):
+        acc = acc + mm(ctx_all[r], cot_all[r - 1], ((0,), (0,)))
+    gw_ref[...] = acc[:share]
+
+    for d in range(4):
+        @pl.when(valid_to[d])
+        def _(d=d):
+            returns[d].wait_recv()
+    grad_ref[...] = (mm(keep_hot, nat[...])
+                     + mm(placing(own_start, own_len), back_recv[...])).astype(BF)
+
+    for c in range(2):
+        own = product(0, c)
+        sent[2 + c].wait_recv()
+        crossing[c].wait_recv()
+        out_ref[:, c * half:(c + 1) * half] = (
+            own + part_in[2 + c].astype(F32) + x_in[c].astype(F32)
+        ).astype(BF)
+
+    for copy in cot_out + [cot_sib] + forward + ctx_out[1:] + gc_out[1:] + sent + crossing:
+        copy.wait_send()
+    for d in range(4):
+        @pl.when(valid_to[d])
+        def _(d=d):
+            images[d].wait_send()
+
+        @pl.when(valid_from[d])
+        def _(d=d):
+            returns[d].wait_send()
+
+
+def local_by_heads(qkv_codes, block_scales, home_segments, kept_rows, pack_list, w_out, cotangent):
+    groups = lax.axis_size("dp")
+    rows = qkv_codes.shape[2]
+    width = qkv_codes.shape[4]
+    model = w_out.shape[1]
+    share = w_out.shape[0]
+    slot = rows // 8
+    feats = 3 * width
+    scales = block_scales[0, 0].reshape(rows, -1)
+    scales = jnp.pad(scales, ((0, 0), (0, 128 - scales.shape[1])))
+    x = jnp.concatenate([qkv_codes[0, 0].reshape(rows, feats), scales], axis=1)
+    vmem = pl.BlockSpec(memory_space=pltpu.VMEM)
+    smem = pl.BlockSpec(memory_space=pltpu.SMEM)
+    dma = pltpu.SemaphoreType.DMA
+    half = model // 2
+    out, grads, gw = pl.pallas_call(
+        functools.partial(heads_kernel, groups, share, width),
+        out_shape=(
+            jax.ShapeDtypeStruct((rows, model), BF),
+            jax.ShapeDtypeStruct((rows, feats), BF),
+            jax.ShapeDtypeStruct((share, model), F32),
+        ),
+        in_specs=[smem, smem, vmem, vmem, vmem, vmem],
+        out_specs=(vmem, vmem, vmem),
+        scratch_shapes=[
+            pltpu.VMEM((4 * slot, feats + 128), BF),
+            pltpu.VMEM((4 * slot, feats + 128), BF),
+            pltpu.VMEM((PAIR, model), BF),
+            pltpu.VMEM((3, rows, model), BF),
+            pltpu.VMEM((rows, feats + 128), BF),
+            pltpu.VMEM((12, rows, PAIR), BF),
+            pltpu.VMEM((12, rows, PAIR), BF),
+            pltpu.VMEM((4, 2 * rows, rows), F32),
+            pltpu.VMEM((4, rows, PAIR), BF),
+            pltpu.VMEM((4, rows, PAIR), BF),
+            pltpu.VMEM((4, rows, PAIR), BF),
+            pltpu.VMEM((4, rows, PAIR), BF),
+            pltpu.VMEM((4, rows, half), BF),
+            pltpu.VMEM((4, rows, half), BF),
+            pltpu.VMEM((2, rows, half), BF),
+            pltpu.VMEM((2, rows, half), BF),
+            pltpu.VMEM((12, rows, PAIR), BF),
+            pltpu.VMEM((rows, feats), BF),
+            pltpu.VMEM((4 * slot, feats), BF),
+            pltpu.VMEM((4 * slot, feats), BF),
+            dma((3,)), dma((3,)), dma((2,)), dma((2,)), dma((4,)), dma((4,)),
+            dma((4,)), dma((4,)), dma((4,)), dma((4,)), dma((4,)), dma((4,)),
+            dma((2,)), dma((2,)), dma((4,)), dma((4,)),
+        ],
+        compiler_params=pltpu.CompilerParams(
+            collective_id=0, has_side_effects=True, vmem_limit_bytes=48 * 1024 * 1024
+        ),
+        cost_estimate=pl.CostEstimate(
+            flops=8 * rows * width * model, bytes_accessed=8 * 1024 * 1024, transcendentals=0
+        ),
+        name="attention_by_heads",
+    )(
+        pack_list[:, 0].reshape(groups, 12),
+        kept_rows,
+        home_segments[0],
+        x,
+        w_out,
+        cotangent[0, 0],
+    )
+    return (out[None, None], grads.reshape(1, 1, rows, 3, width), gw[None])
+
+
 def solution(mesh):
+    fast = mesh.shape["fsdp"] == 4
     return jax.shard_map(
-        local,
+        local_by_heads if fast else local,
         mesh=mesh,
         in_specs=(
             P("dp", "fsdp", None, None, None),

time: 220 us -> 42.8 us (0.19); the launches traced: 216 us -> 42.5 us
  local copies, waits for them, and re-layouts: 106 us -> 8.65 us
  starting transfers between devices: 36 us -> 0 us
  Pallas kernels: 0 us -> 32.5 us
  between operations: 33.2 us -> 1.31 us
  other arithmetic: 16.7 us -> 0.05 us
  matrix products: 15.1 us -> 0 us
  waiting for transfers between devices: 9.6 us -> 0 us
    dynamic_update_slice x12 -> x0, local copies, waits for them, and re-layouts: 78.5 us -> none  [put_rows(): lax.dynamic_update_slice_in_dim(buffer, jnp.where(present, piece, old), a...]
    ppermute x12 -> x0, starting transfers between devices: 35.9 us -> none  [shifted(): return lax.ppermute(block, axis, route)]
    pallas_call x0 -> x1, Pallas kernels: none -> 32.5 us  [local_by_heads(): pl.pallas_call(functools.partial(heads_kernel, groups, share, width), out...]
    dot_general x8 -> x0, matrix products: 13.9 us -> none  [the longest x1 3.37 us: local_layer(): jnp.dot(context, w_full, preferred_element_type=jnp.float32)]
    ppermute x8 -> x0, local copies, waits for them, and re-layouts: 10.7 us -> none  [shifted(): return lax.ppermute(block, axis, route)]
    select_n x19 -> x0, other arithmetic: 10.3 us -> none  [the longest x12 5.34 us: put_rows(): jnp.where(present, piece, old)]
    ppermute x12 -> x0, waiting for transfers between devices: 9.55 us -> none  [shifted(): return lax.ppermute(block, axis, route)]
    select_n x8 -> x0, local copies, waits for them, and re-layouts: 7.34 us -> none  [cut_rows(): return jnp.where(present, piece, jnp.zeros_like(piece))]
  transfers between devices with their start and end apart: 14 -> 0, of which waited for: 3 -> 0; matrix products, arithmetic and copies ran while one was open for 57% -> 0% of each run, Pallas kernels for 0% -> 0%
where the time goes in v1:
time: 42.8 us; the launch traced here: 42.5 us
  Pallas kernels  32.5 us (76%)
  local copies, waits for them, and re-layouts  8.65 us (20%)
  between operations  1.31 us (3%)
    pallas_call x1, Pallas kernels, local_by_heads(): pl.pallas_call(functools.partial(heads_kernel, groups, share, width), out...  32.5 us
    unnamed x10, local copies, waits for them, and re-layouts  6.25 us
    another operation x2, local copies, waits for them, and re-layouts, local_by_heads(): pack_list[:, 0].reshape(groups, 12)  0.87 us

profile of v1, /device:TPU:0, one launch (start us, length us, event | category | flops | bytes accessed | tf_op | source)
XLA Modules:
  0.0 42.5 jit_solution(6256695207977560623)
XLA Ops:
  1.3 0.7 %reshape_squeeze.11 = bf16[128,21]{0,1:T(8,128)(2,1)S(1)} reshape(bf16[1,1,128,3,7]{2,4,3,1,0:T(8,128)(2,1)} %param.8) | data formatting | bytes 10752 | tf_op jit(solution)/shard_map/reshape;squeeze | solution.py:478
  2.0 0.8 %copy.22 = s32[8,1,4,3]{3,2,0,1:T(4,128)S(1)} copy(s32[8,1,4,3]{0,2,3,1:T(4,128)} %param.11) | data formatting | bytes 768 | tf_op jit(solution)/shard_map/reshape;squeeze | solution.py:527
  2.8 0.1 reshape.10.table
  2.8 0.1 copy.17
  3.0 1.4 %copy.16 = bf16[1,1,128,3,896]{2,4,3,1,0:T(8,128)(2,1)S(1)} copy(bf16[1,1,128,3,896]{4,2,3,1,0:T(8,128)(2,1)} %param.7) | data formatting | bytes 1376256 | tf_op args[0]
  4.4 0.0 copy-start.1
  4.4 0.0 copy-start.2
  4.4 0.3 copy.18
  4.8 0.1 fusion.1.x_ref
  4.9 0.6 %copy-done.1 = bf16[1,1,128,1792]{3,2,1,0:T(8,128)(2,1)S(1)} copy-done((bf16[1,1,128,1792]{3,2,1,0:T(8,128)(2,1)S(1)}, bf16[1,1,128,1792]{3,2,1,0:T(8,128)(2,1)}, u32[]{:S(2)}) %copy-start.1) | copy-done | bytes 458776
  5.5 0.0 copy-done.2
  5.5 0.0 copy-start
  5.5 1.1 %copy-done = bf16[224,1792]{1,0:T(8,128)(2,1)S(1)} copy-done((bf16[224,1792]{1,0:T(8,128)(2,1)S(1)}, bf16[224,1792]{1,0:T(8,128)(2,1)}, u32[]{:S(2)}) %copy-start) | copy-done | bytes 802840
  6.6 32.5 %attention_by_heads.1 = (bf16[128,1792]{1,0:T(8,128)(2,1)S(1)}, bf16[128,2688]{1,0:T(8,128)(2,1)S(1)}, f32[224,1792]{1,0:T(8,128)S(1)}) custom-call(s32[8,12]{1,0:T(8,128)S(1)} %reshape.10.table, s32[1,1]{1,0:T(1,128)S(6)} %copy.26.kept_ref, s32[1,128]{1,0:T(1,128)S(1)} %bitcast.13, bf16[128,2816]{1,0:T(8,128)(2,1)S(1)} %fusion.1.x_ref, ...), custom_call_target="tpu_custom_call" | custom-call | flops 1644167168 | bytes 8388608 | tf_op jit(solution)/shard_map/attention_by_heads/pallas_call | solution.py:485
  39.1 0.4 copy.20
  39.4 1.1 %copy.21 = bf16[1,1,128,3,896]{4,2,3,1,0:T(8,128)(2,1)} copy(bf16[1,1,128,3,896]{2,4,3,1,0:T(8,128)(2,1)S(1)} %bitcast.14) | data formatting | bytes 1376256
  40.5 0.8 %copy.27 = bf16[1,1,128,1792]{3,2,1,0:T(8,128)(2,1)} copy(bf16[1,1,128,1792]{3,2,1,0:T(8,128)(2,1)S(1)} %bitcast.11) | data formatting | bytes 917504
  41.3 1.2 %copy.28 = f32[1,224,1792]{2,1,0:T(8,128)} copy(f32[1,224,1792]{2,1,0:T(8,128)S(1)} %bitcast.10) | data formatting | bytes 3211264
Async XLA Ops:
  4.4 1.0 %copy-start.1 = (bf16[1,1,128,1792]{3,2,1,0:T(8,128)(2,1)S(1)}, bf16[1,1,128,1792]{3,2,1,0:T(8,128)(2,1)}, u32[]{:S(2)}) copy-start(bf16[1,1,128,1792]{3,2,1,0:T(8,128)(2,1)} %param.13) | copy-start | bytes 1376260
  4.4 1.0 %copy-start.2 = (s32[1,1,128]{2,1,0:T(1,128)S(1)}, s32[1,1,128]{2,1,0:T(1,128)}, u32[]{:S(2)}) copy-start(s32[1,1,128]{2,1,0:T(1,128)} %param.9) | copy-start | bytes 1540
  5.5 1.1 %copy-start = (bf16[224,1792]{1,0:T(8,128)(2,1)S(1)}, bf16[224,1792]{1,0:T(8,128)(2,1)}, u32[]{:S(2)}) copy-start(bf16[224,1792]{1,0:T(8,128)(2,1)} %w_ref.1) | copy-start | bytes 2408452

commit v2 on v1

--- a/solution.py
+++ b/solution.py
@@ -182,9 +182,9 @@
 
 def heads_kernel(
     groups, share, width,
-    table, kept_ref, seg_ref, x_ref, w_ref, cot_ref,
+    table, kept_ref, seg_ref, scales_ref, codes_hbm, w_hbm, cot_hbm,
     out_ref, grad_ref, gw_ref,
-    img_send, img_recv, w_pad, cot_all, bal, qkv, scl, probs,
+    codes, cot_ref, tall, scal, load_s, img_send, img_recv, w_pad, cot_all, bal, qkv, scl, probs,
     ctx_send, ctx_all, gc_send, gc_in, part_send, part_in, x_send, x_in,
     packed, nat, back_send, back_recv,
     cot_s, cot_r, fwd_s, fwd_r, img_s, img_r, ctx_s, ctx_r, gc_s, gc_r,
@@ -216,6 +216,13 @@
     def at_fsdp(index):
         return (pos, index)
 
+    loads = [
+        pltpu.make_async_copy(codes_hbm, codes, load_s.at[0]),
+        pltpu.make_async_copy(w_hbm, w_pad.at[pl.ds(0, share)], load_s.at[1]),
+        pltpu.make_async_copy(cot_hbm, cot_ref, load_s.at[2]),
+    ]
+    for load in loads:
+        load.start()
     img_recv[...] = jnp.zeros_like(img_recv)
     back_recv[...] = jnp.zeros_like(back_recv)
 
@@ -236,9 +243,9 @@
     cot_out = []
     for c in range(2):
         part = pl.ds(c * hr, hr)
-        cot_out.append(remote(cot_ref.at[part], cot_all.at[1, part], cot_s.at[c], cot_r.at[c],
+        cot_out.append(remote(cot_hbm.at[part], cot_all.at[1, part], cot_s.at[c], cot_r.at[c],
                               at_fsdp(cross)))
-    cot_sib = remote(cot_ref, cot_all.at[0], cot_s.at[2], cot_r.at[2], at_fsdp(sib))
+    cot_sib = remote(cot_hbm, cot_all.at[0], cot_s.at[2], cot_r.at[2], at_fsdp(sib))
     cot_out[0].start()
     cot_out[1].start()
     cot_sib.start()
@@ -260,14 +267,24 @@
             mask = mask + ok.astype(F32)
         return mask.astype(BF)
 
-    own_start = [table[pos, 3 * d] for d in range(4)]
-    own_len = [table[pos, 3 * d + 1] for d in range(4)]
+    own_start = [table[0, d, pos] for d in range(4)]
+    own_len = [table[1, d, pos] for d in range(4)]
     landing, arrived = [], []
     for d in range(4):
         src = jnp.clip(pos - offsets[d], 0, groups - 1)
-        landing.append(table[src, 3 * d + 2])
-        arrived.append(jnp.where(valid_from[d], table[src, 3 * d + 1], 0))
-    img_send[...] = mm(selection(own_start, own_len), x_ref[...]).astype(BF)
+        landing.append(table[2, d, src])
+        arrived.append(jnp.where(valid_from[d], table[1, d, src], 0))
+    tall[...] = jnp.zeros_like(tall)
+    for m in range(3):
+        tall[m * 8:m * 8 + scales_ref.shape[1]] = scales_ref[m].astype(F32)
+    rr = iota((rows, rows), 0)
+    cc = iota((rows, rows), 1)
+    scal[...] = mm(hot(rr == cc), tall[...].astype(BF), ((1,), (1,))).astype(BF)
+    loads[0].wait()
+    chosen = selection(own_start, own_len)
+    for m in range(3):
+        img_send[:, m * width:(m + 1) * width] = mm(chosen, codes[m]).astype(BF)
+    img_send[:, feats:] = mm(chosen, scal[...]).astype(BF)
     images = []
     for d in range(4):
         part = pl.ds(d * slot, slot)
@@ -278,12 +295,11 @@
         def _(d=d):
             images[d].start()
 
-    w_pad[0:share] = w_ref[...]
+    loads[1].wait()
+    loads[2].wait()
     w_pad[share:PAIR] = jnp.zeros((PAIR - share, model), BF)
     gc_in[0] = mm(cot_ref[...], w_pad[...], ((1,), (1,))).astype(BF)
 
-    rr = iota((rows, rows), 0)
-    cc = iota((rows, rows), 1)
     keep_hot = hot((rr == cc) & (rr < kept))
 
     def placing(starts, lengths):
@@ -312,7 +328,10 @@
         def _(d=d):
             images[d].wait_recv()
     place = placing(landing, arrived)
-    bal[...] = (mm(keep_hot, x_ref[...]) + mm(place, img_recv[...])).astype(BF)
+    for m in range(3):
+        part = slice(m * width, (m + 1) * width)
+        bal[:, part] = (mm(keep_hot, codes[m]) + mm(place, img_recv[:, part])).astype(BF)
+    bal[:, feats:] = (mm(keep_hot, scal[...]) + mm(place, img_recv[:, feats:])).astype(BF)
 
     lanes = iota((1, PAIR), 1)
     first = hot(lanes < head)
@@ -324,7 +343,7 @@
         block = (iota((128, PAIR), 1) + j * share) // 128
         for m in range(3):
             values = mm(bal[:, m * width + low:m * width + high], pick)
-            spread = hot((iota((128, PAIR), 0) == block + m * (width // 128))
+            spread = hot((iota((128, PAIR), 0) == block + m * 8)
                          & (iota((128, PAIR), 1) < share))
             scale = mm(bal[:, feats:feats + 128], spread)
             scl[m * 4 + j] = scale.astype(BF)
@@ -444,8 +463,10 @@
         @pl.when(valid_to[d])
         def _(d=d):
             returns[d].wait_recv()
-    grad_ref[...] = (mm(keep_hot, nat[...])
-                     + mm(placing(own_start, own_len), back_recv[...])).astype(BF)
+    place = placing(own_start, own_len)
+    for m in range(3):
+        part = slice(m * width, (m + 1) * width)
+        grad_ref[m] = (mm(keep_hot, nat[:, part]) + mm(place, back_recv[:, part])).astype(BF)
 
     for c in range(2):
         own = product(0, c)
@@ -465,6 +486,17 @@
         @pl.when(valid_from[d])
         def _(d=d):
             returns[d].wait_send()
+
+
+def write_out(a, b, c, a_out, b_out, c_out, sems):
+    copies = [
+        pltpu.make_async_copy(src, dst, sems.at[i])
+        for i, (src, dst) in enumerate(((a, a_out), (b, b_out), (c, c_out)))
+    ]
+    for copy in copies:
+        copy.start()
+    for copy in copies:
+        copy.wait()
 
 
 def local_by_heads(qkv_codes, block_scales, home_segments, kept_rows, pack_list, w_out, cotangent):
@@ -475,10 +507,8 @@
     share = w_out.shape[0]
     slot = rows // 8
     feats = 3 * width
-    scales = block_scales[0, 0].reshape(rows, -1)
-    scales = jnp.pad(scales, ((0, 0), (0, 128 - scales.shape[1])))
-    x = jnp.concatenate([qkv_codes[0, 0].reshape(rows, feats), scales], axis=1)
     vmem = pl.BlockSpec(memory_space=pltpu.VMEM)
+    hbm = pl.BlockSpec(memory_space=pltpu.HBM)
     smem = pl.BlockSpec(memory_space=pltpu.SMEM)
     dma = pltpu.SemaphoreType.DMA
     half = model // 2
@@ -486,12 +516,17 @@
         functools.partial(heads_kernel, groups, share, width),
         out_shape=(
             jax.ShapeDtypeStruct((rows, model), BF),
-            jax.ShapeDtypeStruct((rows, feats), BF),
+            jax.ShapeDtypeStruct((3, rows, width), BF),
             jax.ShapeDtypeStruct((share, model), F32),
         ),
-        in_specs=[smem, smem, vmem, vmem, vmem, vmem],
+        in_specs=[smem, smem, vmem, vmem, hbm, hbm, hbm],
         out_specs=(vmem, vmem, vmem),
         scratch_shapes=[
+            pltpu.VMEM((3, rows, width), BF),
+            pltpu.VMEM((rows, model), BF),
+            pltpu.VMEM((128, rows), F32),
+            pltpu.VMEM((rows, 128), BF),
+            dma((3,)),
             pltpu.VMEM((4 * slot, feats + 128), BF),
             pltpu.VMEM((4 * slot, feats + 128), BF),
             pltpu.VMEM((PAIR, model), BF),
@@ -524,14 +559,25 @@
         ),
         name="attention_by_heads",
     )(
-        pack_list[:, 0].reshape(groups, 12),
+        jnp.transpose(pack_list[:, 0], (2, 1, 0)),
         kept_rows,
         home_segments[0],
-        x,
+        jnp.transpose(block_scales[0, 0], (1, 2, 0)),
+        jnp.transpose(qkv_codes[0, 0], (1, 0, 2)),
         w_out,
         cotangent[0, 0],
     )
-    return (out[None, None], grads.reshape(1, 1, rows, 3, width), gw[None])
+    results = (out, grads, gw)
+    out, grads, gw = pl.pallas_call(
+        write_out,
+        out_shape=tuple(jax.ShapeDtypeStruct(a.shape, a.dtype) for a in results),
+        in_specs=[vmem] * 3,
+        out_specs=(hbm,) * 3,
+        scratch_shapes=[dma((3,))],
+        compiler_params=pltpu.CompilerParams(vmem_limit_bytes=4 * 1024 * 1024),
+        name="write_out",
+    )(*results)
+    return (out[None, None], jnp.transpose(grads, (1, 0, 2))[None, None], gw[None])
 
 
 def solution(mesh):

time: 42.8 us -> 41.6 us (0.972)
  local copies, waits for them, and re-layouts: 8.65 us -> 5.29 us
  Pallas kernels: 32.5 us -> 34.7 us
    another operation x5 -> x0, local copies, waits for them, and re-layouts: 2.05 us -> none  [the longest x2 0.87 us: local_by_heads(): pack_list[:, 0].reshape(groups, 12)]
    pallas_call x0 -> x1, Pallas kernels: none -> 1.56 us  [local_by_heads(): pl.pallas_call(write_out, out_shape=tuple((jax.ShapeDtypeStruct(a.shape,...]
    unnamed x10 -> x12, local copies, waits for them, and re-layouts: 6.25 us -> 5.29 us
    pallas_call x1, Pallas kernels: 32.5 us -> 33.1 us  [local_by_heads(): pl.pallas_call(functools.partial(heads_kernel, groups, share, width), out...]
where the time goes in v2:
time: 41.6 us; the launch traced here: 41.3 us
  Pallas kernels  34.7 us (83%)
  local copies, waits for them, and re-layouts  5.29 us (13%)
  between operations  1.3 us (3%)
    pallas_call x1, Pallas kernels, local_by_heads(): pl.pallas_call(functools.partial(heads_kernel, groups, share, width), out...  33.1 us
    unnamed x12, local copies, waits for them, and re-layouts  5.29 us
    pallas_call x1, Pallas kernels, local_by_heads(): pl.pallas_call(write_out, out_shape=tuple((jax.ShapeDtypeStruct(a.shape,...  1.56 us

profile of v2, /device:TPU:0, one launch (start us, length us, event | category | flops | bytes accessed | tf_op | source)
XLA Modules:
  0.0 41.3 jit_solution(1042549871907363923)
XLA Ops:
  1.3 0.0 copy-start
  1.3 1.1 %copy-done = bf16[224,1792]{1,0:T(8,128)(2,1)S(1)} copy-done((bf16[224,1792]{1,0:T(8,128)(2,1)S(1)}, bf16[224,1792]{1,0:T(8,128)(2,1)}, u32[]{:S(2)}) %copy-start) | copy-done | bytes 802840
  2.4 0.0 copy-start.1
  2.4 1.1 %copy-done.1 = bf16[1,1,128,3,896]{4,2,3,1,0:T(8,128)(2,1)S(1)} copy-done((bf16[1,1,128,3,896]{4,2,3,1,0:T(8,128)(2,1)S(1)}, bf16[1,1,128,3,896]{4,2,3,1,0:T(8,128)(2,1)}, u32[]{:S(2)}) %copy-start.1) | copy-done | bytes 688152
  3.5 0.0 copy-start.2
  3.5 1.0 %copy-done.2 = bf16[1,1,128,1792]{3,2,1,0:T(8,128)(2,1)S(1)} copy-done((bf16[1,1,128,1792]{3,2,1,0:T(8,128)(2,1)S(1)}, bf16[1,1,128,1792]{3,2,1,0:T(8,128)(2,1)}, u32[]{:S(2)}) %copy-start.2) | copy-done | bytes 458776
  4.5 0.0 copy-start.3
  4.5 0.7 %copy-done.3 = s32[8,1,4,3]{0,2,3,1:T(4,128)S(1)} copy-done((s32[8,1,4,3]{0,2,3,1:T(4,128)S(1)}, s32[8,1,4,3]{0,2,3,1:T(4,128)}, u32[]{:S(2)}) %copy-start.3) | copy-done | bytes 408
  5.2 0.0 copy-start.4
  5.2 0.7 %copy-done.4 = bf16[1,1,128,3,7]{2,4,3,1,0:T(8,128)(2,1)S(1)} copy-done((bf16[1,1,128,3,7]{2,4,3,1,0:T(8,128)(2,1)S(1)}, bf16[1,1,128,3,7]{2,4,3,1,0:T(8,128)(2,1)}, u32[]{:S(2)}) %copy-start.4) | copy-done | bytes 5400
  5.9 0.0 copy-start.5
  5.9 0.7 %copy-done.5 = s32[1,1,128]{2,1,0:T(1,128)S(1)} copy-done((s32[1,1,128]{2,1,0:T(1,128)S(1)}, s32[1,1,128]{2,1,0:T(1,128)}, u32[]{:S(2)}) %copy-start.5) | copy-done | bytes 536
  6.6 33.1 %attention_by_heads.1 = (bf16[128,1792]{1,0:T(8,128)(2,1)S(1)}, bf16[3,128,896]{2,1,0:T(8,128)(2,1)S(1)}, f32[224,1792]{1,0:T(8,128)S(1)}) custom-call(s32[3,4,8]{2,1,0:T(4,128)S(1)} %bitcast.18, s32[1,1]{1,0:T(1,128)S(6)} %copy.10.kept_ref, s32[1,128]{1,0:T(1,128)S(1)} %bitcast.20, bf16[3,7,128]{2,1,0:T(8,128)(2,1)S(1)} %bitcast.19, ...), custom_call_target="tpu_custom_call" | custom-call | flops 1644167168 | bytes 8388608 | tf_op jit(solution)/shard_map/attention_by_heads/pallas_call | solution.py:515
  39.7 1.6 %write_out.1 = (bf16[128,1792]{1,0:T(8,128)(2,1)}, bf16[3,128,896]{2,1,0:T(8,128)(2,1)}, f32[224,1792]{1,0:T(8,128)}) custom-call(bf16[128,1792]{1,0:T(8,128)(2,1)S(1)} %get-tuple-element.9.a, bf16[3,128,896]{2,1,0:T(8,128)(2,1)S(1)} %get-tuple-element.10.b, f32[224,1792]{1,0:T(8,128)S(1)} %get-tuple-element.11.c), custom_call_target="tpu_custom_call" | custom-call | tf_op jit(solution)/shard_map/write_out/pallas_call | solution.py:571
Async XLA Ops:
  1.3 1.1 %copy-start = (bf16[224,1792]{1,0:T(8,128)(2,1)S(1)}, bf16[224,1792]{1,0:T(8,128)(2,1)}, u32[]{:S(2)}) copy-start(bf16[224,1792]{1,0:T(8,128)(2,1)} %w_hbm.1) | copy-start | bytes 2408452
  2.4 1.1 %copy-start.1 = (bf16[1,1,128,3,896]{4,2,3,1,0:T(8,128)(2,1)S(1)}, bf16[1,1,128,3,896]{4,2,3,1,0:T(8,128)(2,1)}, u32[]{:S(2)}) copy-start(bf16[1,1,128,3,896]{4,2,3,1,0:T(8,128)(2,1)} %param.7) | copy-start | bytes 2064388
  3.5 1.0 %copy-start.2 = (bf16[1,1,128,1792]{3,2,1,0:T(8,128)(2,1)S(1)}, bf16[1,1,128,1792]{3,2,1,0:T(8,128)(2,1)}, u32[]{:S(2)}) copy-start(bf16[1,1,128,1792]{3,2,1,0:T(8,128)(2,1)} %param.13) | copy-start | bytes 1376260
  4.5 0.7 %copy-start.3 = (s32[8,1,4,3]{0,2,3,1:T(4,128)S(1)}, s32[8,1,4,3]{0,2,3,1:T(4,128)}, u32[]{:S(2)}) copy-start(s32[8,1,4,3]{0,2,3,1:T(4,128)} %param.11) | copy-start | bytes 1156
  5.2 0.7 %copy-start.4 = (bf16[1,1,128,3,7]{2,4,3,1,0:T(8,128)(2,1)S(1)}, bf16[1,1,128,3,7]{2,4,3,1,0:T(8,128)(2,1)}, u32[]{:S(2)}) copy-start(bf16[1,1,128,3,7]{2,4,3,1,0:T(8,128)(2,1)} %param.8) | copy-start | bytes 16132
  5.9 0.7 %copy-start.5 = (s32[1,1,128]{2,1,0:T(1,128)S(1)}, s32[1,1,128]{2,1,0:T(1,128)}, u32[]{:S(2)}) copy-start(s32[1,1,128]{2,1,0:T(1,128)} %param.9) | copy-start | bytes 1540

commit v3 on v2

--- a/solution.py
+++ b/solution.py
@@ -515,9 +515,9 @@
     out, grads, gw = pl.pallas_call(
         functools.partial(heads_kernel, groups, share, width),
         out_shape=(
-            jax.ShapeDtypeStruct((rows, model), BF),
-            jax.ShapeDtypeStruct((3, rows, width), BF),
-            jax.ShapeDtypeStruct((share, model), F32),
+            pltpu.VMEM((rows, model), BF),
+            pltpu.VMEM((3, rows, width), BF),
+            pltpu.VMEM((share, model), F32),
         ),
         in_specs=[smem, smem, vmem, vmem, hbm, hbm, hbm],
         out_specs=(vmem, vmem, vmem),
@@ -552,7 +552,7 @@
             dma((2,)), dma((2,)), dma((4,)), dma((4,)),
         ],
         compiler_params=pltpu.CompilerParams(
-            collective_id=0, has_side_effects=True, vmem_limit_bytes=48 * 1024 * 1024
+            collective_id=0, has_side_effects=True, vmem_limit_bytes=58 * 1024 * 1024
         ),
         cost_estimate=pl.CostEstimate(
             flops=8 * rows * width * model, bytes_accessed=8 * 1024 * 1024, transcendentals=0

time: 41.6 us -> 35.9 us (0.86)
  local copies, waits for them, and re-layouts: 5.29 us -> 0 us
    unnamed x12 -> x0, local copies, waits for them, and re-layouts: 5.29 us -> none
where the time goes in v3:
time: 35.9 us; the launch traced here: 35.7 us
  Pallas kernels  34.4 us (96%)
  between operations  1.29 us (4%)
    pallas_call x1, Pallas kernels, local_by_heads(): pl.pallas_call(functools.partial(heads_kernel, groups, share, width), out...  32.8 us
    pallas_call x1, Pallas kernels, local_by_heads(): pl.pallas_call(write_out, out_shape=tuple((jax.ShapeDtypeStruct(a.shape,...  1.56 us

profile of v3, /device:TPU:0, one launch (start us, length us, event | category | flops | bytes accessed | tf_op | source)
XLA Modules:
  0.0 35.7 jit_solution(7438409580793784836)
XLA Ops:
  1.3 32.8 %attention_by_heads.1 = (bf16[128,1792]{1,0:T(8,128)(2,1)S(1)}, bf16[3,128,896]{2,1,0:T(8,128)(2,1)S(1)}, f32[224,1792]{1,0:T(8,128)S(1)}) custom-call(s32[3,4,8]{2,1,0:T(4,128)} %bitcast.21, s32[1,1]{1,0:T(1,128)S(6)} %copy.10.kept_ref, s32[1,128]{1,0:T(1,128)} %bitcast.23, bf16[3,7,128]{2,1,0:T(8,128)(2,1)} %bitcast.22, bf16[3,128,896]{2,1,0:T(8,128)(2,1)} %bitcast.17, ...), custom_call_target="tpu_custom_call" | custom-call | flops 1644167168 | bytes 8388608 | tf_op jit(solution)/shard_map/attention_by_heads/pallas_call | solution.py:515
  34.1 1.6 %write_out.1 = (bf16[128,1792]{1,0:T(8,128)(2,1)}, bf16[3,128,896]{2,1,0:T(8,128)(2,1)}, f32[224,1792]{1,0:T(8,128)}) custom-call(bf16[128,1792]{1,0:T(8,128)(2,1)S(1)} %get-tuple-element.9.a, bf16[3,128,896]{2,1,0:T(8,128)(2,1)S(1)} %get-tuple-element.10.b, f32[224,1792]{1,0:T(8,128)S(1)} %get-tuple-element.11.c), custom_call_target="tpu_custom_call" | custom-call | tf_op jit(solution)/shard_map/write_out/pallas_call | solution.py:571

commit v4 on v3

--- a/solution.py
+++ b/solution.py
@@ -184,11 +184,10 @@
     groups, share, width,
     table, kept_ref, seg_ref, scales_ref, codes_hbm, w_hbm, cot_hbm,
     out_ref, grad_ref, gw_ref,
-    codes, cot_ref, tall, scal, load_s, img_send, img_recv, w_pad, cot_all, bal, qkv, scl, probs,
-    ctx_send, ctx_all, gc_send, gc_in, part_send, part_in, x_send, x_in,
-    packed, nat, back_send, back_recv,
-    cot_s, cot_r, fwd_s, fwd_r, img_s, img_r, ctx_s, ctx_r, gc_s, gc_r,
-    part_s, part_r, xs_s, xs_r, back_s, back_r,
+    codes, tall, scal, img_send, img_recv, w_all, cot_all, bal, qkv, scl, probs,
+    ctx_own, ctx_all, packed, nat, back_send, back_recv,
+    load_s, cot_s, cot_r, fwd_s, fwd_r, img_s, img_r, ctx_s, ctx_r, back_s, back_r,
+    wsib_s, wsib_r, wx_s, wx_r, wq_s, wq_r, wf_s, wf_r,
 ):
     pos = lax.axis_index("dp")
     me = lax.axis_index("fsdp")
@@ -196,11 +195,11 @@
     cross = (me + 2) % 4
     diag = (sib + 2) % 4
     peer = (me, sib, cross, diag)
-    rows = cot_ref.shape[0]
+    quad = pos % 4
+    rows = cot_hbm.shape[0]
     slot = img_send.shape[0] // 4
     feats = 3 * width
-    model = cot_ref.shape[1]
-    half = model // 2
+    model = cot_hbm.shape[1]
     head = width // HEADS
     factor = 1.0 / math.sqrt(head)
 
@@ -218,8 +217,8 @@
 
     loads = [
         pltpu.make_async_copy(codes_hbm, codes, load_s.at[0]),
-        pltpu.make_async_copy(w_hbm, w_pad.at[pl.ds(0, share)], load_s.at[1]),
-        pltpu.make_async_copy(cot_hbm, cot_ref, load_s.at[2]),
+        pltpu.make_async_copy(w_hbm, w_all.at[0, pl.ds(0, share)], load_s.at[1]),
+        pltpu.make_async_copy(cot_hbm, cot_all.at[0], load_s.at[2]),
     ]
     for load in loads:
         load.start()
@@ -237,20 +236,52 @@
         def _(d=d):
             pl.semaphore_signal(barrier, inc=1, device_id=at_dp(pos + offsets[d]),
                                 device_id_type=pl.DeviceIdType.MESH)
-    pl.semaphore_wait(barrier, 3 + jnp.minimum(pos, 2) + jnp.minimum(groups - 1 - pos, 2))
+    far = pos + 3 - 2 * quad
+    outer = (quad == 0) | (quad == 3)
+
+    @pl.when(outer)
+    def _():
+        pl.semaphore_signal(barrier, inc=1, device_id=at_dp(far),
+                            device_id_type=pl.DeviceIdType.MESH)
+    pl.semaphore_wait(barrier, 3 + jnp.minimum(pos, 2) + jnp.minimum(groups - 1 - pos, 2)
+                      + outer.astype(jnp.int32))
+
+    tiles = model // 128
+    cuts = [tiles * i // 4 * 128 for i in range(5)]
+
+    def columns(ref, r, i):
+        return ref.at[r, pl.ds(0, share), pl.ds(cuts[i], cuts[i + 1] - cuts[i])]
+
+    w_sib = remote(w_hbm, w_all.at[1, pl.ds(0, share)], wsib_s, wsib_r, at_fsdp(sib))
+    w_cross = [
+        remote(w_hbm.at[:, pl.ds(cuts[i], cuts[i + 1] - cuts[i])], columns(w_all, 2, i),
+               wx_s.at[i], wx_r.at[i], at_fsdp(cross))
+        for i in range(4)
+    ]
+    w_quad = [
+        [remote(columns(w_all, 2, i), columns(w_all, 2, i), wq_s.at[4 * i + p], wq_r.at[i],
+                at_dp(pos - quad + p)) for p in range(4)]
+        for i in range(4)
+    ]
+    w_fwd = [
+        remote(columns(w_all, 2, i), columns(w_all, 3, i), wf_s.at[i], wf_r.at[i], at_fsdp(sib))
+        for i in range(4)
+    ]
+    for i in range(4):
+        @pl.when(quad == i)
+        def _(i=i):
+            w_cross[i].start()
+    w_sib.start()
 
     hr = rows // 2
-    cot_out = []
-    for c in range(2):
-        part = pl.ds(c * hr, hr)
-        cot_out.append(remote(cot_hbm.at[part], cot_all.at[1, part], cot_s.at[c], cot_r.at[c],
-                              at_fsdp(cross)))
-    cot_sib = remote(cot_hbm, cot_all.at[0], cot_s.at[2], cot_r.at[2], at_fsdp(sib))
-    cot_out[0].start()
-    cot_out[1].start()
-    cot_sib.start()
+    cot_out = [
+        remote(cot_hbm.at[pl.ds(c * hr, hr)], cot_all.at[2, pl.ds(c * hr, hr)],
+               cot_s.at[c], cot_r.at[c], at_fsdp(cross))
+        for c in range(2)
+    ]
+    cot_sib = remote(cot_hbm, cot_all.at[1], cot_s.at[2], cot_r.at[2], at_fsdp(sib))
     forward = [
-        remote(cot_all.at[1, pl.ds(c * hr, hr)], cot_all.at[2, pl.ds(c * hr, hr)],
+        remote(cot_all.at[2, pl.ds(c * hr, hr)], cot_all.at[3, pl.ds(c * hr, hr)],
                fwd_s.at[c], fwd_r.at[c], at_fsdp(sib))
         for c in range(2)
     ]
@@ -297,8 +328,9 @@
 
     loads[1].wait()
     loads[2].wait()
-    w_pad[share:PAIR] = jnp.zeros((PAIR - share, model), BF)
-    gc_in[0] = mm(cot_ref[...], w_pad[...], ((1,), (1,))).astype(BF)
+    for r in range(4):
+        w_all[r, share:PAIR] = jnp.zeros((PAIR - share, model), BF)
+    gc_own = mm(cot_all[0], w_all[0], ((1,), (1,))).astype(BF)
 
     keep_hot = hot((rr == cc) & (rr < kept))
 
@@ -322,6 +354,17 @@
     same = marks_col == marks_row
     bias = jnp.where(same, 0.0, -jnp.inf)
     bias2 = jnp.concatenate([bias, bias], axis=0)
+
+    for i in range(4):
+        @pl.when(quad == i)
+        def _(i=i):
+            w_cross[i].wait_recv()
+            for p in range(4):
+                if p != i:
+                    w_quad[i][p].start()
+            w_fwd[i].start()
+    for copy in cot_out + [cot_sib]:
+        copy.start()
 
     for d in range(4):
         @pl.when(valid_from[d])
@@ -364,62 +407,18 @@
         p = weights / jnp.sum(weights, axis=-1, keepdims=True)
         probs[r] = p
         ctx = mm(wide(p.astype(BF)), stack(qkv[8 + j])).astype(BF)
+        ctx_own[r] = ctx
         if r == 0:
             ctx_all[0] = ctx
         else:
-            ctx_send[r] = ctx
-            ctx_out[r] = remote(ctx_send.at[r], ctx_all.at[r], ctx_s.at[r], ctx_r.at[r],
+            ctx_out[r] = remote(ctx_own.at[r], ctx_all.at[r], ctx_s.at[r], ctx_r.at[r],
                                 at_fsdp(j))
             ctx_out[r].start()
 
-    gc_out = [None] * 4
-
-    def send_gc(r):
-        gc_send[r] = mm(cot_all[r - 1], w_pad[...], ((1,), (1,))).astype(BF)
-        gc_out[r] = remote(gc_send.at[r], gc_in.at[r], gc_s.at[r], gc_r.at[r], at_fsdp(peer[r]))
-        gc_out[r].start()
-
-    cot_sib.wait_recv()
-    for c in range(2):
-        cot_out[c].wait_recv()
-        forward[c].start()
-    send_gc(2)
-    send_gc(1)
-    for c in range(2):
-        forward[c].wait_recv()
-    send_gc(3)
-
-    def product(r, c):
-        return mm(ctx_all[r], w_pad[:, c * half:(c + 1) * half])
-
-    sent = []
-    crossing = []
-    ctx_out[3].wait_recv()
-    for c in range(2):
-        part_send[c] = product(3, c).astype(BF)
-        sent.append(remote(part_send.at[c], part_in.at[c], part_s.at[c], part_r.at[c],
-                           at_fsdp(sib)))
-        sent[c].start()
-    ctx_out[2].wait_recv()
-    for c in range(2):
-        own = product(2, c)
-        sent[c].wait_recv()
-        x_send[c] = (own + part_in[c].astype(F32)).astype(BF)
-        crossing.append(remote(x_send.at[c], x_in.at[c], xs_s.at[c], xs_r.at[c], at_fsdp(cross)))
-        crossing[c].start()
-    ctx_out[1].wait_recv()
-    for c in range(2):
-        part_send[2 + c] = product(1, c).astype(BF)
-        sent.append(remote(part_send.at[2 + c], part_in.at[2 + c], part_s.at[2 + c],
-                           part_r.at[2 + c], at_fsdp(sib)))
-        sent[2 + c].start()
-
-    for r in (0, 1, 2, 3):
+    def backward(r, gc):
         j = peer[r]
-        if r:
-            gc_out[r].wait_recv()
         p = probs[r]
-        gstack = stack(gc_in[r])
+        gstack = stack(gc)
         gp = mm(gstack, qkv[8 + j], ((1,), (1,)))
         total = jnp.sum(p * gp, axis=-1, keepdims=True)
         gs = (p * (gp - total) * factor).astype(BF)
@@ -428,6 +427,22 @@
         gv = mm(p.astype(BF), gstack, ((0,), (0,)))
         for m, g in enumerate((gq, gk, gv)):
             packed[m * 4 + j] = (g * scl[m * 4 + j].astype(F32)).astype(BF)
+
+    def gradient(r):
+        return mm(cot_all[0], w_all[r], ((1,), (1,))).astype(BF)
+
+    backward(0, gc_own)
+    w_sib.wait_recv()
+    backward(1, gradient(1))
+    for i in range(4):
+        @pl.when(quad != i)
+        def _(i=i):
+            w_quad[i][i].wait_recv()
+            w_fwd[i].start()
+    backward(2, gradient(2))
+    for i in range(4):
+        w_fwd[i].wait_recv()
+    backward(3, gradient(3))
     for m in range(3):
         blocks = [None] * (width // 128)
         for j in range(4):
@@ -454,10 +469,19 @@
         def _(d=d):
             returns[d].start()
 
-    acc = mm(ctx_all[0], cot_ref[...], ((0,), (0,)))
+    out_ref[...] = mm(jnp.concatenate([ctx_own[r] for r in range(4)], axis=1),
+                      w_all[...].reshape(4 * PAIR, model)).astype(BF)
+
+    for c in range(2):
+        cot_out[c].wait_recv()
+        forward[c].start()
+    cot_sib.wait_recv()
     for r in (1, 2, 3):
-        acc = acc + mm(ctx_all[r], cot_all[r - 1], ((0,), (0,)))
-    gw_ref[...] = acc[:share]
+        ctx_out[r].wait_recv()
+    for c in range(2):
+        forward[c].wait_recv()
+    gw_ref[...] = mm(ctx_all[...].reshape(4 * rows, PAIR), cot_all[...].reshape(4 * rows, model),
+                     ((0,), (0,)))[:share]
 
     for d in range(4):
         @pl.when(valid_to[d])
@@ -468,16 +492,15 @@
         part = slice(m * width, (m + 1) * width)
         grad_ref[m] = (mm(keep_hot, nat[:, part]) + mm(place, back_recv[:, part])).astype(BF)
 
-    for c in range(2):
-        own = product(0, c)
-        sent[2 + c].wait_recv()
-        crossing[c].wait_recv()
-        out_ref[:, c * half:(c + 1) * half] = (
-            own + part_in[2 + c].astype(F32) + x_in[c].astype(F32)
-        ).astype(BF)
-
-    for copy in cot_out + [cot_sib] + forward + ctx_out[1:] + gc_out[1:] + sent + crossing:
+    for copy in cot_out + [cot_sib, w_sib] + forward + w_fwd + ctx_out[1:]:
         copy.wait_send()
+    for i in range(4):
+        @pl.when(quad == i)
+        def _(i=i):
+            w_cross[i].wait_send()
+            for p in range(4):
+                if p != i:
+                    w_quad[i][p].wait_send()
     for d in range(4):
         @pl.when(valid_to[d])
         def _(d=d):
@@ -511,7 +534,6 @@
     hbm = pl.BlockSpec(memory_space=pltpu.HBM)
     smem = pl.BlockSpec(memory_space=pltpu.SMEM)
     dma = pltpu.SemaphoreType.DMA
-    half = model // 2
     out, grads, gw = pl.pallas_call(
         functools.partial(heads_kernel, groups, share, width),
         out_shape=(
@@ -523,33 +545,25 @@
         out_specs=(vmem, vmem, vmem),
         scratch_shapes=[
             pltpu.VMEM((3, rows, width), BF),
-            pltpu.VMEM((rows, model), BF),
             pltpu.VMEM((128, rows), F32),
             pltpu.VMEM((rows, 128), BF),
-            dma((3,)),
             pltpu.VMEM((4 * slot, feats + 128), BF),
             pltpu.VMEM((4 * slot, feats + 128), BF),
-            pltpu.VMEM((PAIR, model), BF),
-            pltpu.VMEM((3, rows, model), BF),
+            pltpu.VMEM((4, PAIR, model), BF),
+            pltpu.VMEM((4, rows, model), BF),
             pltpu.VMEM((rows, feats + 128), BF),
             pltpu.VMEM((12, rows, PAIR), BF),
             pltpu.VMEM((12, rows, PAIR), BF),
             pltpu.VMEM((4, 2 * rows, rows), F32),
             pltpu.VMEM((4, rows, PAIR), BF),
             pltpu.VMEM((4, rows, PAIR), BF),
-            pltpu.VMEM((4, rows, PAIR), BF),
-            pltpu.VMEM((4, rows, PAIR), BF),
-            pltpu.VMEM((4, rows, half), BF),
-            pltpu.VMEM((4, rows, half), BF),
-            pltpu.VMEM((2, rows, half), BF),
-            pltpu.VMEM((2, rows, half), BF),
             pltpu.VMEM((12, rows, PAIR), BF),
             pltpu.VMEM((rows, feats), BF),
             pltpu.VMEM((4 * slot, feats), BF),
             pltpu.VMEM((4 * slot, feats), BF),
-            dma((3,)), dma((3,)), dma((2,)), dma((2,)), dma((4,)), dma((4,)),
-            dma((4,)), dma((4,)), dma((4,)), dma((4,)), dma((4,)), dma((4,)),
-            dma((2,)), dma((2,)), dma((4,)), dma((4,)),
+            dma((3,)), dma((3,)), dma((3,)), dma((2,)), dma((2,)), dma((4,)), dma((4,)),
+            dma((4,)), dma((4,)), dma((4,)), dma((4,)),
+            dma, dma, dma((4,)), dma((4,)), dma((16,)), dma((4,)), dma((4,)), dma((4,)),
         ],
         compiler_params=pltpu.CompilerParams(
             collective_id=0, has_side_effects=True, vmem_limit_bytes=58 * 1024 * 1024
@@ -581,7 +595,7 @@
 
 
 def solution(mesh):
-    fast = mesh.shape["fsdp"] == 4
+    fast = mesh.shape["fsdp"] == 4 and mesh.shape["dp"] % 4 == 0
     return jax.shard_map(
         local_by_heads if fast else local,
         mesh=mesh,

time: 35.9 us -> 35.8 us (level)
  no operation moved by 1% of the time
where the time goes in v4:
time: 35.8 us; the launch traced here: 35.6 us
  Pallas kernels  34.3 us (96%)
  between operations  1.29 us (4%)
    pallas_call x1, Pallas kernels, local_by_heads(): pl.pallas_call(functools.partial(heads_kernel, groups, share, width), out...  32.7 us
    pallas_call x1, Pallas kernels, local_by_heads(): pl.pallas_call(write_out, out_shape=tuple((jax.ShapeDtypeStruct(a.shape,...  1.56 us

profile of v4, /device:TPU:0, one launch (start us, length us, event | category | flops | bytes accessed | tf_op | source)
XLA Modules:
  0.0 35.6 jit_solution(13307448805714369650)
XLA Ops:
  1.3 32.7 %attention_by_heads.1 = (bf16[128,1792]{1,0:T(8,128)(2,1)S(1)}, bf16[3,128,896]{2,1,0:T(8,128)(2,1)S(1)}, f32[224,1792]{1,0:T(8,128)S(1)}) custom-call(s32[3,4,8]{2,1,0:T(4,128)} %bitcast.21, s32[1,1]{1,0:T(1,128)S(6)} %copy.10.kept_ref, s32[1,128]{1,0:T(1,128)} %bitcast.23, bf16[3,7,128]{2,1,0:T(8,128)(2,1)} %bitcast.22, bf16[3,128,896]{2,1,0:T(8,128)(2,1)} %bitcast.17, ...), custom_call_target="tpu_custom_call" | custom-call | flops 1644167168 | bytes 8388608 | tf_op jit(solution)/shard_map/attention_by_heads/pallas_call | solution.py:537
  34.0 1.6 %write_out.1 = (bf16[128,1792]{1,0:T(8,128)(2,1)}, bf16[3,128,896]{2,1,0:T(8,128)(2,1)}, f32[224,1792]{1,0:T(8,128)}) custom-call(bf16[128,1792]{1,0:T(8,128)(2,1)S(1)} %get-tuple-element.9.a, bf16[3,128,896]{2,1,0:T(8,128)(2,1)S(1)} %get-tuple-element.10.b, f32[224,1792]{1,0:T(8,128)S(1)} %get-tuple-element.11.c), custom_call_target="tpu_custom_call" | custom-call | tf_op jit(solution)/shard_map/write_out/pallas_call | solution.py:585

commit v5 on v4

--- a/solution.py
+++ b/solution.py
@@ -249,28 +249,34 @@
     tiles = model // 128
     cuts = [tiles * i // 4 * 128 for i in range(5)]
 
-    def columns(ref, r, i):
-        return ref.at[r, pl.ds(0, share), pl.ds(cuts[i], cuts[i + 1] - cuts[i])]
+    split = share // 2 // 16 * 16
+    bands = ((0, split), (split, share - split))
+    pieces = [(i, c) for i in range(4) for c in range(2)]
+
+    def columns(ref, i, c):
+        return ref.at[pl.ds(*bands[c]), pl.ds(cuts[i], cuts[i + 1] - cuts[i])]
 
     w_sib = remote(w_hbm, w_all.at[1, pl.ds(0, share)], wsib_s, wsib_r, at_fsdp(sib))
-    w_cross = [
-        remote(w_hbm.at[:, pl.ds(cuts[i], cuts[i + 1] - cuts[i])], columns(w_all, 2, i),
-               wx_s.at[i], wx_r.at[i], at_fsdp(cross))
-        for i in range(4)
-    ]
-    w_quad = [
-        [remote(columns(w_all, 2, i), columns(w_all, 2, i), wq_s.at[4 * i + p], wq_r.at[i],
-                at_dp(pos - quad + p)) for p in range(4)]
-        for i in range(4)
-    ]
-    w_fwd = [
-        remote(columns(w_all, 2, i), columns(w_all, 3, i), wf_s.at[i], wf_r.at[i], at_fsdp(sib))
-        for i in range(4)
-    ]
+    w_cross = {
+        (i, c): remote(columns(w_hbm, i, c), columns(w_all.at[2], i, c),
+                       wx_s.at[2 * i + c], wx_r.at[2 * i + c], at_fsdp(cross))
+        for i, c in pieces
+    }
+    w_quad = {
+        (i, c, p): remote(columns(w_all.at[2], i, c), columns(w_all.at[2], i, c),
+                          wq_s.at[8 * i + 4 * c + p], wq_r.at[2 * i + c], at_dp(pos - quad + p))
+        for i, c in pieces for p in range(4)
+    }
+    w_fwd = {
+        (i, c): remote(columns(w_all.at[2], i, c), columns(w_all.at[3], i, c),
+                       wf_s.at[2 * i + c], wf_r.at[2 * i + c], at_fsdp(sib))
+        for i, c in pieces
+    }
     for i in range(4):
         @pl.when(quad == i)
         def _(i=i):
-            w_cross[i].start()
+            w_cross[i, 0].start()
+            w_cross[i, 1].start()
     w_sib.start()
 
     hr = rows // 2
@@ -326,13 +332,38 @@
         def _(d=d):
             images[d].start()
 
+    def hand_on(c):
+        for i in range(4):
+            @pl.when(quad == i)
+            def _(i=i):
+                w_cross[i, c].wait_recv()
+                for p in range(4):
+                    if p != i:
+                        w_quad[i, c, p].start()
+                w_fwd[i, c].start()
+
+    hand_on(0)
+
     loads[1].wait()
     loads[2].wait()
     for r in range(4):
         w_all[r, share:PAIR] = jnp.zeros((PAIR - share, model), BF)
     gc_own = mm(cot_all[0], w_all[0], ((1,), (1,))).astype(BF)
 
-    keep_hot = hot((rr == cc) & (rr < kept))
+    keep = iota((rows, 1), 0) < kept
+    lanes = iota((1, PAIR), 1)
+    first = hot(lanes < head)
+    second = hot(lanes >= head)
+    picks = []
+    spreads = [None] * 12
+    for j in range(4):
+        low, high = window(j, share)
+        picks.append(hot((iota((high - low, PAIR), 0) + low
+                          == iota((high - low, PAIR), 1) + j * share)
+                         & (iota((high - low, PAIR), 1) < share)))
+        block = jnp.where(lanes < share, (lanes + j * share) // 128, -128)
+        for m in range(3):
+            spreads[m * 4 + j] = hot(iota((128, PAIR), 0) == block + m * 8)
 
     def placing(starts, lengths):
         r_ = iota((rows, 4 * slot), 0)
@@ -355,14 +386,7 @@
     bias = jnp.where(same, 0.0, -jnp.inf)
     bias2 = jnp.concatenate([bias, bias], axis=0)
 
-    for i in range(4):
-        @pl.when(quad == i)
-        def _(i=i):
-            w_cross[i].wait_recv()
-            for p in range(4):
-                if p != i:
-                    w_quad[i][p].start()
-            w_fwd[i].start()
+    hand_on(1)
     for copy in cot_out + [cot_sib]:
         copy.start()
 
@@ -373,22 +397,14 @@
     place = placing(landing, arrived)
     for m in range(3):
         part = slice(m * width, (m + 1) * width)
-        bal[:, part] = (mm(keep_hot, codes[m]) + mm(place, img_recv[:, part])).astype(BF)
-    bal[:, feats:] = (mm(keep_hot, scal[...]) + mm(place, img_recv[:, feats:])).astype(BF)
-
-    lanes = iota((1, PAIR), 1)
-    first = hot(lanes < head)
-    second = hot(lanes >= head)
+        bal[:, part] = jnp.where(keep, codes[m], mm(place, img_recv[:, part]).astype(BF))
+    bal[:, feats:] = jnp.where(keep, scal[...], mm(place, img_recv[:, feats:]).astype(BF))
+
     for j in range(4):
         low, high = window(j, share)
-        pick = hot((iota((high - low, PAIR), 0) + low == iota((high - low, PAIR), 1) + j * share)
-                   & (iota((high - low, PAIR), 1) < share))
-        block = (iota((128, PAIR), 1) + j * share) // 128
         for m in range(3):
-            values = mm(bal[:, m * width + low:m * width + high], pick)
-            spread = hot((iota((128, PAIR), 0) == block + m * 8)
-                         & (iota((128, PAIR), 1) < share))
-            scale = mm(bal[:, feats:feats + 128], spread)
+            values = mm(bal[:, m * width + low:m * width + high], picks[j])
+            scale = mm(bal[:, feats:feats + 128], spreads[m * 4 + j])
             scl[m * 4 + j] = scale.astype(BF)
             qkv[m * 4 + j] = (values * scale).astype(BF)
 
@@ -398,8 +414,9 @@
     def wide(x):
         return jnp.concatenate([x[:rows], x[rows:]], axis=1)
 
+    w_sib.wait_recv()
     ctx_out = [None] * 4
-    for r in (2, 3, 1, 0):
+    for r in range(4):
         j = peer[r]
         scores = mm(stack(qkv[j]), qkv[4 + j], ((1,), (1,))) * factor + bias2
         top = jnp.max(scores, axis=-1, keepdims=True)
@@ -413,7 +430,6 @@
         else:
             ctx_out[r] = remote(ctx_own.at[r], ctx_all.at[r], ctx_s.at[r], ctx_r.at[r],
                                 at_fsdp(j))
-            ctx_out[r].start()
 
     def backward(r, gc):
         j = peer[r]
@@ -432,16 +448,17 @@
         return mm(cot_all[0], w_all[r], ((1,), (1,))).astype(BF)
 
     backward(0, gc_own)
-    w_sib.wait_recv()
     backward(1, gradient(1))
-    for i in range(4):
+    for r in (1, 2, 3):
+        ctx_out[r].start()
+    for i, c in sorted(pieces, key=lambda piece: piece[1]):
         @pl.when(quad != i)
-        def _(i=i):
-            w_quad[i][i].wait_recv()
-            w_fwd[i].start()
+        def _(i=i, c=c):
+            w_quad[i, c, i].wait_recv()
+            w_fwd[i, c].start()
+    for piece in pieces:
+        w_fwd[piece].wait_recv()
     backward(2, gradient(2))
-    for i in range(4):
-        w_fwd[i].wait_recv()
     backward(3, gradient(3))
     for m in range(3):
         blocks = [None] * (width // 128)
@@ -490,17 +507,18 @@
     place = placing(own_start, own_len)
     for m in range(3):
         part = slice(m * width, (m + 1) * width)
-        grad_ref[m] = (mm(keep_hot, nat[:, part]) + mm(place, back_recv[:, part])).astype(BF)
-
-    for copy in cot_out + [cot_sib, w_sib] + forward + w_fwd + ctx_out[1:]:
+        grad_ref[m] = jnp.where(keep, nat[:, part], mm(place, back_recv[:, part]).astype(BF))
+
+    for copy in cot_out + [cot_sib, w_sib] + forward + list(w_fwd.values()) + ctx_out[1:]:
         copy.wait_send()
     for i in range(4):
         @pl.when(quad == i)
         def _(i=i):
-            w_cross[i].wait_send()
-            for p in range(4):
-                if p != i:
-                    w_quad[i][p].wait_send()
+            for c in range(2):
+                w_cross[i, c].wait_send()
+                for p in range(4):
+                    if p != i:
+                        w_quad[i, c, p].wait_send()
     for d in range(4):
         @pl.when(valid_to[d])
         def _(d=d):
@@ -563,7 +581,7 @@
             pltpu.VMEM((4 * slot, feats), BF),
             dma((3,)), dma((3,)), dma((3,)), dma((2,)), dma((2,)), dma((4,)), dma((4,)),
             dma((4,)), dma((4,)), dma((4,)), dma((4,)),
-            dma, dma, dma((4,)), dma((4,)), dma((16,)), dma((4,)), dma((4,)), dma((4,)),
+            dma, dma, dma((8,)), dma((8,)), dma((32,)), dma((8,)), dma((8,)), dma((8,)),
         ],
         compiler_params=pltpu.CompilerParams(
             collective_id=0, has_side_effects=True, vmem_limit_bytes=58 * 1024 * 1024

time: 35.8 us -> 33.9 us (0.947)
  Pallas kernels: 34.3 us -> 32.4 us
    pallas_call x1, Pallas kernels: 32.7 us -> 30.8 us  [local_by_heads(): pl.pallas_call(functools.partial(heads_kernel, groups, share, width), out...]
where the time goes in v5:
time: 33.9 us; the launch traced here: 33.7 us
  Pallas kernels  32.4 us (96%)
  between operations  1.29 us (4%)
    pallas_call x1, Pallas kernels, local_by_heads(): pl.pallas_call(functools.partial(heads_kernel, groups, share, width), out...  30.8 us
    pallas_call x1, Pallas kernels, local_by_heads(): pl.pallas_call(write_out, out_shape=tuple((jax.ShapeDtypeStruct(a.shape,...  1.56 us

profile of v5, /device:TPU:0, one launch (start us, length us, event | category | flops | bytes accessed | tf_op | source)
XLA Modules:
  0.0 33.7 jit_solution(15539139264194988013)
XLA Ops:
  1.3 30.8 %attention_by_heads.1 = (bf16[128,1792]{1,0:T(8,128)(2,1)S(1)}, bf16[3,128,896]{2,1,0:T(8,128)(2,1)S(1)}, f32[224,1792]{1,0:T(8,128)S(1)}) custom-call(s32[3,4,8]{2,1,0:T(4,128)} %bitcast.21, s32[1,1]{1,0:T(1,128)S(6)} %copy.10.kept_ref, s32[1,128]{1,0:T(1,128)} %bitcast.23, bf16[3,7,128]{2,1,0:T(8,128)(2,1)} %bitcast.22, bf16[3,128,896]{2,1,0:T(8,128)(2,1)} %bitcast.17, ...), custom_call_target="tpu_custom_call" | custom-call | flops 1644167168 | bytes 8388608 | tf_op jit(solution)/shard_map/attention_by_heads/pallas_call | solution.py:555
  32.1 1.6 %write_out.1 = (bf16[128,1792]{1,0:T(8,128)(2,1)}, bf16[3,128,896]{2,1,0:T(8,128)(2,1)}, f32[224,1792]{1,0:T(8,128)}) custom-call(bf16[128,1792]{1,0:T(8,128)(2,1)S(1)} %get-tuple-element.9.a, bf16[3,128,896]{2,1,0:T(8,128)(2,1)S(1)} %get-tuple-element.10.b, f32[224,1792]{1,0:T(8,128)S(1)} %get-tuple-element.11.c), custom_call_target="tpu_custom_call" | custom-call | tf_op jit(solution)/shard_map/write_out/pallas_call | solution.py:603

commit v6 on v5

--- a/solution.py
+++ b/solution.py
@@ -185,7 +185,7 @@
     table, kept_ref, seg_ref, scales_ref, codes_hbm, w_hbm, cot_hbm,
     out_ref, grad_ref, gw_ref,
     codes, tall, scal, img_send, img_recv, w_all, cot_all, bal, qkv, scl, probs,
-    ctx_own, ctx_all, packed, nat, back_send, back_recv,
+    out_acc, ctx_own, ctx_all, packed, nat, back_send, back_recv,
     load_s, cot_s, cot_r, fwd_s, fwd_r, img_s, img_r, ctx_s, ctx_r, back_s, back_r,
     wsib_s, wsib_r, wx_s, wx_r, wq_s, wq_r, wf_s, wf_r,
 ):
@@ -337,9 +337,8 @@
             @pl.when(quad == i)
             def _(i=i):
                 w_cross[i, c].wait_recv()
-                for p in range(4):
-                    if p != i:
-                        w_quad[i, c, p].start()
+                for step in (1, 2, 3):
+                    w_quad[i, c, i ^ step].start()
                 w_fwd[i, c].start()
 
     hand_on(0)
@@ -451,6 +450,19 @@
     backward(1, gradient(1))
     for r in (1, 2, 3):
         ctx_out[r].start()
+
+    def projected(r):
+        return mm(jnp.concatenate([ctx_own[r], ctx_own[r + 1]], axis=1),
+                  w_all[r:r + 2].reshape(2 * PAIR, model))
+
+    def weight_terms(r):
+        return mm(ctx_all[r:r + 2].reshape(2 * rows, PAIR),
+                  cot_all[r:r + 2].reshape(2 * rows, model), ((0,), (0,)))[:share]
+
+    out_acc[...] = projected(0)
+    cot_sib.wait_recv()
+    ctx_out[1].wait_recv()
+    gw_ref[...] = weight_terms(0)
     for i, c in sorted(pieces, key=lambda piece: piece[1]):
         @pl.when(quad != i)
         def _(i=i, c=c):
@@ -486,19 +498,16 @@
         def _(d=d):
             returns[d].start()
 
-    out_ref[...] = mm(jnp.concatenate([ctx_own[r] for r in range(4)], axis=1),
-                      w_all[...].reshape(4 * PAIR, model)).astype(BF)
+    out_ref[...] = (out_acc[...] + projected(2)).astype(BF)
 
     for c in range(2):
         cot_out[c].wait_recv()
         forward[c].start()
-    cot_sib.wait_recv()
-    for r in (1, 2, 3):
+    for r in (2, 3):
         ctx_out[r].wait_recv()
     for c in range(2):
         forward[c].wait_recv()
-    gw_ref[...] = mm(ctx_all[...].reshape(4 * rows, PAIR), cot_all[...].reshape(4 * rows, model),
-                     ((0,), (0,)))[:share]
+    gw_ref[...] += weight_terms(2)
 
     for d in range(4):
         @pl.when(valid_to[d])
@@ -573,6 +582,7 @@
             pltpu.VMEM((12, rows, PAIR), BF),
             pltpu.VMEM((12, rows, PAIR), BF),
             pltpu.VMEM((4, 2 * rows, rows), F32),
+            pltpu.VMEM((rows, model), F32),
             pltpu.VMEM((4, rows, PAIR), BF),
             pltpu.VMEM((4, rows, PAIR), BF),
             pltpu.VMEM((12, rows, PAIR), BF),

time: 33.9 us -> 33.9 us (level)
  no operation moved by 1% of the time
where the time goes in v6:
time: 33.9 us; the launch traced here: 33.5 us
  Pallas kernels  32.2 us (95%)
  between operations  1.29 us (4%)
    pallas_call x1, Pallas kernels, local_by_heads(): pl.pallas_call(functools.partial(heads_kernel, groups, share, width), out...  30.7 us
    pallas_call x1, Pallas kernels, local_by_heads(): pl.pallas_call(write_out, out_shape=tuple((jax.ShapeDtypeStruct(a.shape,...  1.56 us

profile of v6, /device:TPU:0, one launch (start us, length us, event | category | flops | bytes accessed | tf_op | source)
XLA Modules:
  0.0 33.5 jit_solution(5250893587837827751)
XLA Ops:
  1.3 30.7 %attention_by_heads.1 = (bf16[128,1792]{1,0:T(8,128)(2,1)S(1)}, bf16[3,128,896]{2,1,0:T(8,128)(2,1)S(1)}, f32[224,1792]{1,0:T(8,128)S(1)}) custom-call(s32[3,4,8]{2,1,0:T(4,128)} %bitcast.21, s32[1,1]{1,0:T(1,128)S(6)} %copy.10.kept_ref, s32[1,128]{1,0:T(1,128)} %bitcast.23, bf16[3,7,128]{2,1,0:T(8,128)(2,1)} %bitcast.22, bf16[3,128,896]{2,1,0:T(8,128)(2,1)} %bitcast.17, ...), custom_call_target="tpu_custom_call" | custom-call | flops 1644167168 | bytes 8388608 | tf_op jit(solution)/shard_map/attention_by_heads/pallas_call | solution.py:564
  32.0 1.6 %write_out.1 = (bf16[128,1792]{1,0:T(8,128)(2,1)}, bf16[3,128,896]{2,1,0:T(8,128)(2,1)}, f32[224,1792]{1,0:T(8,128)}) custom-call(bf16[128,1792]{1,0:T(8,128)(2,1)S(1)} %get-tuple-element.9.a, bf16[3,128,896]{2,1,0:T(8,128)(2,1)S(1)} %get-tuple-element.10.b, f32[224,1792]{1,0:T(8,128)S(1)} %get-tuple-element.11.c), custom_call_target="tpu_custom_call" | custom-call | tf_op jit(solution)/shard_map/write_out/pallas_call | solution.py:613

commit v7 on v6

--- a/solution.py
+++ b/solution.py
@@ -185,7 +185,7 @@
     table, kept_ref, seg_ref, scales_ref, codes_hbm, w_hbm, cot_hbm,
     out_ref, grad_ref, gw_ref,
     codes, tall, scal, img_send, img_recv, w_all, cot_all, bal, qkv, scl, probs,
-    out_acc, ctx_own, ctx_all, packed, nat, back_send, back_recv,
+    out_acc, ctx_own, ctx_all, packed, back_send, back_recv,
     load_s, cot_s, cot_r, fwd_s, fwd_r, img_s, img_r, ctx_s, ctx_r, back_s, back_r,
     wsib_s, wsib_r, wx_s, wx_r, wq_s, wq_r, wf_s, wf_r,
 ):
@@ -446,10 +446,40 @@
     def gradient(r):
         return mm(cot_all[0], w_all[r], ((1,), (1,))).astype(BF)
 
+    going = selection(landing, arrived)
+    returns = {
+        (h, d): remote(back_send.at[h, pl.ds(d * slot, slot)],
+                       back_recv.at[h, pl.ds(d * slot, slot)],
+                       back_s.at[4 * h + d], back_r.at[4 * h + d],
+                       at_dp(jnp.clip(pos - offsets[d], 0, groups - 1)))
+        for h in range(2) for d in range(4)
+    }
+    parts = [(m, k, slice((2 * m + k) * PAIR, (2 * m + k + 1) * PAIR))
+             for m in range(3) for k in range(2)]
+
+    def send_back(h):
+        for m, k, cols in parts:
+            back_send[h, :, cols] = mm(going, packed[m * 4 + peer[2 * h + k]]).astype(BF)
+        for d in range(4):
+            @pl.when(valid_from[d])
+            def _(d=d):
+                returns[h, d].start()
+
+    def bring_home(h):
+        for d in range(4):
+            @pl.when(valid_to[d])
+            def _(d=d):
+                returns[h, d].wait_recv()
+        for m, k, cols in parts:
+            at = m * 4 + peer[2 * h + k]
+            placed = mm(home, back_recv[h, :, cols]).astype(BF)
+            packed[at] = jnp.where(keep, packed[at], placed)
+
     backward(0, gc_own)
     backward(1, gradient(1))
     for r in (1, 2, 3):
         ctx_out[r].start()
+    send_back(0)
 
     def projected(r):
         return mm(jnp.concatenate([ctx_own[r], ctx_own[r + 1]], axis=1),
@@ -472,6 +502,23 @@
         w_fwd[piece].wait_recv()
     backward(2, gradient(2))
     backward(3, gradient(3))
+    send_back(1)
+
+    out_ref[...] = (out_acc[...] + projected(2)).astype(BF)
+
+    home = placing(own_start, own_len)
+    bring_home(0)
+
+    for c in range(2):
+        cot_out[c].wait_recv()
+        forward[c].start()
+    for r in (2, 3):
+        ctx_out[r].wait_recv()
+    for c in range(2):
+        forward[c].wait_recv()
+    gw_ref[...] += weight_terms(2)
+
+    bring_home(1)
     for m in range(3):
         blocks = [None] * (width // 128)
         for j in range(4):
@@ -485,38 +532,7 @@
                 at = low // 128 + b
                 blocks[at] = add if blocks[at] is None else blocks[at] + add
         for b in range(width // 128):
-            nat[:, m * width + b * 128:m * width + (b + 1) * 128] = blocks[b].astype(BF)
-
-    back_send[...] = mm(selection(landing, arrived), nat[...]).astype(BF)
-    returns = []
-    for d in range(4):
-        part = pl.ds(d * slot, slot)
-        returns.append(remote(back_send.at[part], back_recv.at[part], back_s.at[d], back_r.at[d],
-                              at_dp(jnp.clip(pos - offsets[d], 0, groups - 1))))
-
-        @pl.when(valid_from[d])
-        def _(d=d):
-            returns[d].start()
-
-    out_ref[...] = (out_acc[...] + projected(2)).astype(BF)
-
-    for c in range(2):
-        cot_out[c].wait_recv()
-        forward[c].start()
-    for r in (2, 3):
-        ctx_out[r].wait_recv()
-    for c in range(2):
-        forward[c].wait_recv()
-    gw_ref[...] += weight_terms(2)
-
-    for d in range(4):
-        @pl.when(valid_to[d])
-        def _(d=d):
-            returns[d].wait_recv()
-    place = placing(own_start, own_len)
-    for m in range(3):
-        part = slice(m * width, (m + 1) * width)
-        grad_ref[m] = jnp.where(keep, nat[:, part], mm(place, back_recv[:, part]).astype(BF))
+            grad_ref[m, :, b * 128:(b + 1) * 128] = blocks[b].astype(BF)
 
     for copy in cot_out + [cot_sib, w_sib] + forward + list(w_fwd.values()) + ctx_out[1:]:
         copy.wait_send()
@@ -535,7 +551,8 @@
 
         @pl.when(valid_from[d])
         def _(d=d):
-            returns[d].wait_send()
+            returns[0, d].wait_send()
+            returns[1, d].wait_send()
 
 
 def write_out(a, b, c, a_out, b_out, c_out, sems):
@@ -586,11 +603,10 @@
             pltpu.VMEM((4, rows, PAIR), BF),
             pltpu.VMEM((4, rows, PAIR), BF),
             pltpu.VMEM((12, rows, PAIR), BF),
-            pltpu.VMEM((rows, feats), BF),
-            pltpu.VMEM((4 * slot, feats), BF),
-            pltpu.VMEM((4 * slot, feats), BF),
+            pltpu.VMEM((2, 4 * slot, 6 * PAIR), BF),
+            pltpu.VMEM((2, 4 * slot, 6 * PAIR), BF),
             dma((3,)), dma((3,)), dma((3,)), dma((2,)), dma((2,)), dma((4,)), dma((4,)),
-            dma((4,)), dma((4,)), dma((4,)), dma((4,)),
+            dma((4,)), dma((4,)), dma((8,)), dma((8,)),
             dma, dma, dma((8,)), dma((8,)), dma((32,)), dma((8,)), dma((8,)), dma((8,)),
         ],
         compiler_params=pltpu.CompilerParams(

time: 33.9 us -> 33.4 us (0.985)
  Pallas kernels: 32.2 us -> 31.7 us
    pallas_call x1, Pallas kernels: 30.7 us -> 30.1 us  [local_by_heads(): pl.pallas_call(functools.partial(heads_kernel, groups, share, width), out...]
where the time goes in v7:
time: 33.4 us; the launch traced here: 33 us
  Pallas kernels  31.7 us (95%)
  between operations  1.29 us (4%)
    pallas_call x1, Pallas kernels, local_by_heads(): pl.pallas_call(functools.partial(heads_kernel, groups, share, width), out...  30.1 us
    pallas_call x1, Pallas kernels, local_by_heads(): pl.pallas_call(write_out, out_shape=tuple((jax.ShapeDtypeStruct(a.shape,...  1.56 us

profile of v7, /device:TPU:0, one launch (start us, length us, event | category | flops | bytes accessed | tf_op | source)
XLA Modules:
  0.0 33.0 jit_solution(14267843699724570746)
XLA Ops:
  1.3 30.1 %attention_by_heads.1 = (bf16[128,1792]{1,0:T(8,128)(2,1)S(1)}, bf16[3,128,896]{2,1,0:T(8,128)(2,1)S(1)}, f32[224,1792]{1,0:T(8,128)S(1)}) custom-call(s32[3,4,8]{2,1,0:T(4,128)} %bitcast.21, s32[1,1]{1,0:T(1,128)S(6)} %copy.10.kept_ref, s32[1,128]{1,0:T(1,128)} %bitcast.23, bf16[3,7,128]{2,1,0:T(8,128)(2,1)} %bitcast.22, bf16[3,128,896]{2,1,0:T(8,128)(2,1)} %bitcast.17, ...), custom_call_target="tpu_custom_call" | custom-call | flops 1644167168 | bytes 8388608 | tf_op jit(solution)/shard_map/attention_by_heads/pallas_call | solution.py:581
  31.4 1.6 %write_out.1 = (bf16[128,1792]{1,0:T(8,128)(2,1)}, bf16[3,128,896]{2,1,0:T(8,128)(2,1)}, f32[224,1792]{1,0:T(8,128)}) custom-call(bf16[128,1792]{1,0:T(8,128)(2,1)S(1)} %get-tuple-element.9.a, bf16[3,128,896]{2,1,0:T(8,128)(2,1)S(1)} %get-tuple-element.10.b, f32[224,1792]{1,0:T(8,128)S(1)} %get-tuple-element.11.c), custom_call_target="tpu_custom_call" | custom-call | tf_op jit(solution)/shard_map/write_out/pallas_call | solution.py:629

commit v8 on v7

--- a/solution.py
+++ b/solution.py
@@ -430,6 +430,9 @@
             ctx_out[r] = remote(ctx_own.at[r], ctx_all.at[r], ctx_s.at[r], ctx_r.at[r],
                                 at_fsdp(j))
 
+    for r in (1, 2, 3):
+        ctx_out[r].start()
+
     def backward(r, gc):
         j = peer[r]
         p = probs[r]
@@ -477,8 +480,6 @@
 
     backward(0, gc_own)
     backward(1, gradient(1))
-    for r in (1, 2, 3):
-        ctx_out[r].start()
     send_back(0)
 
     def projected(r):

time: 33.4 us -> 33.4 us (level)
  no operation moved by 1% of the time
where the time goes in v8:
time: 33.4 us; the launch traced here: 33 us
  Pallas kernels  31.7 us (95%)
  between operations  1.29 us (4%)
    pallas_call x1, Pallas kernels, local_by_heads(): pl.pallas_call(functools.partial(heads_kernel, groups, share, width), out...  30.1 us
    pallas_call x1, Pallas kernels, local_by_heads(): pl.pallas_call(write_out, out_shape=tuple((jax.ShapeDtypeStruct(a.shape,...  1.56 us

profile of v8, /device:TPU:0, one launch (start us, length us, event | category | flops | bytes accessed | tf_op | source)
XLA Modules:
  0.0 33.0 jit_solution(12645757053994367355)
XLA Ops:
  1.3 30.1 %attention_by_heads.1 = (bf16[128,1792]{1,0:T(8,128)(2,1)S(1)}, bf16[3,128,896]{2,1,0:T(8,128)(2,1)S(1)}, f32[224,1792]{1,0:T(8,128)S(1)}) custom-call(s32[3,4,8]{2,1,0:T(4,128)} %bitcast.21, s32[1,1]{1,0:T(1,128)S(6)} %copy.10.kept_ref, s32[1,128]{1,0:T(1,128)} %bitcast.23, bf16[3,7,128]{2,1,0:T(8,128)(2,1)} %bitcast.22, bf16[3,128,896]{2,1,0:T(8,128)(2,1)} %bitcast.17, ...), custom_call_target="tpu_custom_call" | custom-call | flops 1644167168 | bytes 8388608 | tf_op jit(solution)/shard_map/attention_by_heads/pallas_call | solution.py:582
  31.4 1.6 %write_out.1 = (bf16[128,1792]{1,0:T(8,128)(2,1)}, bf16[3,128,896]{2,1,0:T(8,128)(2,1)}, f32[224,1792]{1,0:T(8,128)}) custom-call(bf16[128,1792]{1,0:T(8,128)(2,1)S(1)} %get-tuple-element.9.a, bf16[3,128,896]{2,1,0:T(8,128)(2,1)S(1)} %get-tuple-element.10.b, f32[224,1792]{1,0:T(8,128)S(1)} %get-tuple-element.11.c), custom_call_target="tpu_custom_call" | custom-call | tf_op jit(solution)/shard_map/write_out/pallas_call | solution.py:630
